TPU v7x, 32 devices: a whole 2x2x4 slice. The times are simulated.
32 devices in a mesh: dp: 2 (over x), lat: 4 (over y, core), lon: 4 (over z).
Axes of the slice: x: 2, y: 2, z: 4, core: 2. Of those that a mesh axis runs over, the one named last changes fastest.
Arguments:
- inputs: bfloat16 [2, 128, 64, 1024], P('dp', 'lat', 'lon'), may hold values from -40 to 40
- grad_out: bfloat16 [2, 128, 64, 1024], P('dp', 'lat', 'lon'), may hold values from -6 to 6
- w_qkv: bfloat16 [1024, 3072], replicated, may hold values from -0.1875 to 0.1875
Outputs:
- grad_inputs: bfloat16 [2, 128, 64, 1024], P('dp', 'lat', 'lon')
- grad_w_qkv: float32 [1024, 3072], P(('dp', 'lat', 'lon'))
All inputs are finite; a program needn't handle non-finite values.
Results may differ from a plain program's by a relative error of at most 0.011.
Values may be sent and summed in bfloat16 or wider, within the bound.
No kernel may reach another device: no remote copies, remote signals or barrier semaphores. Data moves between devices by JAX's collectives and lax.ppermute only.
A program may use at most 192 MiB of HBM per device.

v0:
```python
import functools

import jax
import jax.numpy as jnp
import numpy as np
from jax import lax
from jax.experimental import pallas as pl
from jax.experimental.pallas import tpu as pltpu
from jax.sharding import PartitionSpec as P

HEADS = 16
WIN = 13
MARGIN = WIN // 2
TILE_R = 4
GROUP = 4
KEY_COLS = 32
HALO_COLS = 16
REGION_R = 16
PAD_R = 2
EDGE_R = MARGIN + PAD_R
NEG = -1e30
BF = jnp.bfloat16
F32 = jnp.float32
MIB = 1024 * 1024
GATHER_FLOPS = 4 * 10**9
FINISH_FLOPS = 9 * 10**9
LANES = 128
ATTENTION_MIB = 46

NT = (((1,), (1,)), ((), ()))
TN = (((0,), (0,)), ((), ()))
NN = (((1,), (0,)), ((), ()))


def dot(a, b, dims=NN):
    return lax.dot_general(a, b, dims, preferred_element_type=F32)


def region_top(tile, band_start, band_rows, total_rows):
    lowest = jnp.where(band_start == 0, TILE_R, 0)
    highest = jnp.where(band_start + band_rows == total_rows, band_rows - 2 * TILE_R, band_rows)
    return jnp.clip(tile * TILE_R, lowest, highest)


def mask_kernel(band_rows, band_cols, total_rows, start_ref, mask_ref):
    band_start = start_ref[0]
    tile = pl.program_id(0)
    shape = mask_ref.shape[1:]
    first = region_top(tile, band_start, band_rows, total_rows)
    key = lax.broadcasted_iota(jnp.int32, shape, 0)
    query = lax.broadcasted_iota(jnp.int32, shape, 1) & (TILE_R * band_cols - 1)
    key_row = band_start - MARGIN + first + (key >> (KEY_COLS.bit_length() - 1))
    place = key & (KEY_COLS - 1)
    query_row = band_start + tile * TILE_R + (query >> (band_cols.bit_length() - 1))
    query_col = query & (band_cols - 1)
    window = jnp.clip(query_row - MARGIN, 0, total_rows - WIN)
    row_inside = (key_row >= window) & (key_row < window + WIN)
    key_col = jnp.where(
        place < band_cols,
        place,
        jnp.where(place < band_cols + MARGIN, place - band_cols - MARGIN, place - MARGIN),
    )
    col_inside = (jnp.abs(key_col - query_col) <= MARGIN) & (place < band_cols + 2 * MARGIN)
    mask_ref[0] = jnp.where(row_inside & col_inside, 0.0, NEG).astype(BF)


def window_masks(start, band_rows, band_cols, total_rows):
    tiles = band_rows // TILE_R
    shape = (REGION_R * KEY_COLS, 2 * TILE_R * band_cols)
    return pl.pallas_call(
        functools.partial(mask_kernel, band_rows, band_cols, total_rows),
        grid=(tiles,),
        in_specs=[pl.BlockSpec(memory_space=pltpu.SMEM)],
        out_specs=pl.BlockSpec((1,) + shape, lambda t: (t, 0, 0)),
        out_shape=jax.ShapeDtypeStruct((tiles,) + shape, BF),
        cost_estimate=pl.CostEstimate(flops=10**7, bytes_accessed=2**21, transcendentals=0),
    )(start)


def attention_kernel(band_rows, band_cols, total_rows, head_width, extra, first, count, *refs):
    (place_ref, mask_ref, left_ref, right_ref, rows_a, rows_b, corners_a, corners_b,
     qkv_hbm, grad_hbm, w_hbm) = refs[:11]
    (dq_ref, out_a, out_b, mid_ref, to_left_ref, to_right_ref,
     halo_ref, spot_ref, q_ref, k_ref, v_ref, dk_ref, dv_ref,
     own_refs, w_refs, own_sem, w_sem) = refs[11 + extra :]
    band_start = place_ref[0]
    even = place_ref[1] == 0
    tiles = band_rows // TILE_R
    queries = TILE_R * band_cols
    keys = REGION_R * KEY_COLS
    width = GROUP * head_width
    lanes = GROUP * queries
    region_rows = band_rows + 2 * MARGIN
    side = MARGIN * band_rows
    edge = MARGIN * band_cols
    corner = 2 * MARGIN * EDGE_R
    at_above = 2 * side
    at_below = at_above + edge
    at_cl = at_below + edge
    at_cr = at_cl + corner
    halves = [(i, slice(i * LANES, (i + 1) * LANES)) for i in range(width // LANES)]

    step = pl.program_id(0)
    groups = HEADS // GROUP

    def copies(slot, parts):
        at = lambda part: pl.ds((part * groups + first + slot) * width, width)
        for part, source, where, i in parts:
            target, sem = (w_refs, w_sem) if where else (own_refs, own_sem)
            yield pltpu.make_async_copy(source.at[:, at(part)], target.at[slot, i], sem.at[slot, i])

    for_k = ((1, w_hbm, 1, 0), (1, qkv_hbm, 0, 1))
    for_v = ((2, w_hbm, 1, 1), (2, qkv_hbm, 0, 2))
    for_q = ((0, qkv_hbm, 0, 0), (0, grad_hbm, 0, 3))

    def await_copies(parts):
        for slot in range(count):

            @pl.when(step == slot)
            def _():
                for copy in copies(slot, parts):
                    copy.wait()

    @pl.when(step == 0)
    def _():
        for slot in range(count):
            for copy in copies(slot, for_k + for_v + for_q):
                copy.start()
        halo_ref[:side] = left_ref[...]
        halo_ref[side:at_above] = right_ref[...]
        for above, below, size, refs_ab in (
            (at_above, at_below, edge, (rows_a, rows_b)),
            (at_cl, at_cr, corner, (corners_a, corners_b)),
        ):
            for ref, at in zip(refs_ab, (jnp.where(even, below, above), jnp.where(even, above, below))):
                halo_ref[pl.ds(pl.multiple_of(at, 16), size), :] = ref[...]
        spot_ref[...] = jnp.zeros_like(spot_ref)

    def place(target, own, weights):
        fresh = dot(halo_ref[...], weights)
        for col in range(MARGIN):
            start = MARGIN * HALO_COLS + col
            for part, at in halves:
                spot_ref[part, pl.ds(start, band_rows, stride=HALO_COLS), :] = fresh[
                    col * band_rows : (col + 1) * band_rows, at
                ]
                spot_ref[part, pl.ds(start + MARGIN, band_rows, stride=HALO_COLS), :] = fresh[
                    side + col * band_rows : side + (col + 1) * band_rows, at
                ]
        for corner_at, skip, row in ((at_cl, PAD_R, 0), (at_cr, 0, MARGIN + band_rows)):
            for col in range(2 * MARGIN):
                base = corner_at + col * EDGE_R + skip
                spot = pl.ds(row * HALO_COLS + col, MARGIN, stride=HALO_COLS)
                for part, at in halves:
                    spot_ref[part, spot, :] = fresh[base : base + MARGIN, at]
        for row in range(region_rows):
            base = row * KEY_COLS
            inner = row - MARGIN
            if inner < 0:
                ours = fresh[at_above + row * band_cols : at_above + (row + 1) * band_cols].astype(BF)
            elif inner < band_rows:
                ours = own[inner * band_cols : (inner + 1) * band_cols, :]
            else:
                past = at_below + (inner - band_rows) * band_cols
                ours = fresh[past : past + band_cols].astype(BF)
            target[base : base + band_cols, :] = ours
            for part, at in halves:
                target[base + band_cols : base + KEY_COLS, at] = spot_ref[
                    part, row * HALO_COLS : (row + 1) * HALO_COLS, :
                ].astype(BF)

    grad_ref = own_refs.at[step, 3]
    await_copies(for_k)
    place(k_ref, own_refs.at[step, 1], w_refs[step, 0])
    await_copies(for_v)
    place(v_ref, own_refs.at[step, 2], w_refs[step, 1])
    await_copies(for_q)
    q_ref[...] = own_refs[step, 0] * BF(head_width**-0.5)
    dk_ref[...] = jnp.zeros_like(dk_ref)
    dv_ref[...] = jnp.zeros_like(dv_ref)

    def spread(rows):
        block = jnp.concatenate([rows] * GROUP, axis=0)
        head_row = lax.broadcasted_iota(jnp.int32, (lanes, width), 0) // queries
        head_col = lax.broadcasted_iota(jnp.int32, (lanes, width), 1) // head_width
        return jnp.where(head_row == head_col, block, jnp.zeros_like(block))

    def one_tile(tile, carry):
        first = region_top(tile, band_start, band_rows, total_rows)
        region = pl.ds(pl.multiple_of(first * KEY_COLS, TILE_R * KEY_COLS), keys)
        total = pl.ds(pl.multiple_of((first + PAD_R) * KEY_COLS, PAD_R * KEY_COLS), keys)
        mine = pl.ds(pl.multiple_of(tile * queries, queries), queries)
        q_wide = spread(q_ref[mine, :])
        g_wide = spread(grad_ref[mine, :])
        mask = mask_ref[tile].astype(F32)
        scores = dot(k_ref[region, :], q_wide, NT) + jnp.concatenate([mask, mask], axis=1)
        dots = dot(v_ref[region, :], g_wide, NT)
        exponent = jnp.exp(scores - jnp.max(scores, axis=0, keepdims=True))
        inverse = 1.0 / jnp.sum(exponent, axis=0, keepdims=True)
        delta = jnp.sum(exponent * dots, axis=0, keepdims=True) * inverse
        attn = exponent * inverse
        dscore = (attn * (dots - delta)).astype(BF)
        dv = dot(attn.astype(BF), g_wide)
        dk = dot(dscore, q_wide)
        for part, at in halves:
            dv_ref[part, total, :] += dv[:, at]
            dk_ref[part, total, :] += dk[:, at]
        dq_wide = dot(dscore, k_ref[region, :], TN)
        head_col = lax.broadcasted_iota(jnp.int32, (queries, width), 1) // head_width
        dq = jnp.zeros((queries, width), F32)
        for head in range(GROUP):
            dq = jnp.where(head_col == head, dq_wide[head * queries : (head + 1) * queries], dq)
        dq_ref[mine, :] = (dq * head_width**-0.5).astype(BF)
        return carry

    lax.fori_loop(0, tiles, one_tile, 0, unroll=4)

    middle = (PAD_R + MARGIN) * KEY_COLS
    below = (PAD_R + MARGIN + band_rows) * KEY_COLS
    for part, acc in enumerate((dk_ref, dv_ref)):
        for lane, at in halves:
            for out, own_at, side_at in (
                (out_a, jnp.where(even, below, PAD_R * KEY_COLS), jnp.where(even, below, 0)),
                (out_b, jnp.where(even, PAD_R * KEY_COLS, below), jnp.where(even, 0, below)),
            ):
                for row in range(MARGIN):
                    start = pl.multiple_of(own_at + row * KEY_COLS, KEY_COLS)
                    out[part, row * band_cols : (row + 1) * band_cols, at] = acc[
                        lane, pl.ds(start, band_cols), :
                    ].astype(BF)
                for pair in range(MARGIN):
                    here = slice(edge + pair * 2 * EDGE_R, edge + (pair + 1) * 2 * EDGE_R)
                    start = side_at + band_cols + 2 * pair
                    out[part, here, at] = jnp.concatenate(
                        [
                            acc[lane, pl.ds(start, EDGE_R, stride=KEY_COLS), :],
                            acc[lane, pl.ds(start + 1, EDGE_R, stride=KEY_COLS), :],
                        ],
                        axis=0,
                    ).astype(BF)
            for row in range(band_rows):
                base = middle + row * KEY_COLS
                mid_ref[part, row * band_cols : (row + 1) * band_cols, at] = acc[
                    lane, base : base + band_cols, :
                ].astype(BF)
            for col in range(MARGIN):
                here = slice(col * band_rows, (col + 1) * band_rows)
                start = middle + band_cols + col
                to_left_ref[part, here, at] = acc[
                    lane, pl.ds(start, band_rows, stride=KEY_COLS), :
                ].astype(BF)
                to_right_ref[part, here, at] = acc[
                    lane, pl.ds(start + MARGIN, band_rows, stride=KEY_COLS), :
                ].astype(BF)


def attention_grads(
    first, count, slots, start, masks, halo, qkv, grad_out, w_qkv, shape, before, after
):
    band_rows, band_cols, total_rows = shape
    tokens, width = grad_out.shape
    head_width = width // HEADS
    block = GROUP * head_width
    region_tokens = (band_rows + 2 * MARGIN) * KEY_COLS
    total_tokens = (band_rows + 2 * MARGIN + 2 * PAD_R) * KEY_COLS
    side = MARGIN * band_rows
    edge = MARGIN * (band_cols + 2 * EDGE_R)
    corner = 2 * MARGIN * EDGE_R
    halo_tokens = 2 * (side + MARGIN * band_cols + corner)
    whole = lambda g: (0, 0)
    column = lambda offset: (lambda g: (0, offset + first + g))
    slot = lambda g: (0, 0, first % slots + g)
    halves = [(2, edge), (2, edge), (2, tokens), (2, side), (2, side)]
    out_shape = [jax.ShapeDtypeStruct((tokens, width), BF)] + [
        jax.ShapeDtypeStruct(s + (slots * block,), BF) for s in halves
    ]
    aliases = {}
    if before:
        aliases = {11 + i: place for i, (place, _) in enumerate(before)}
    return pl.pallas_call(
        functools.partial(
            attention_kernel, band_rows, band_cols, total_rows, head_width,
            len(before) + len(after), first, count,
        ),
        grid=(count,),
        in_specs=[
            pl.BlockSpec(memory_space=pltpu.SMEM),
            pl.BlockSpec(masks.shape, lambda g: (0, 0, 0)),
        ]
        + [pl.BlockSpec(piece.shape, whole) for piece in halo]
        + [pl.BlockSpec(memory_space=pltpu.HBM)] * 3
        + [pl.BlockSpec(memory_space=pl.ANY)] * (len(before) + len(after)),
        out_specs=[pl.BlockSpec((tokens, block), column(0))]
        + [pl.BlockSpec(s + (block,), slot) for s in halves],
        out_shape=out_shape,
        input_output_aliases=aliases,
        scratch_shapes=[
            pltpu.VMEM((halo_tokens, width), BF),
            pltpu.VMEM((block // LANES, (band_rows + 2 * MARGIN) * HALO_COLS, LANES), F32),
            pltpu.VMEM((tokens, block), BF),
            pltpu.VMEM((region_tokens, block), BF),
            pltpu.VMEM((region_tokens, block), BF),
            pltpu.VMEM((block // LANES, total_tokens, LANES), F32),
            pltpu.VMEM((block // LANES, total_tokens, LANES), F32),
            pltpu.VMEM((count, 4, tokens, block), BF),
            pltpu.VMEM((count, 2, width, block), BF),
            pltpu.SemaphoreType.DMA((count, 4)),
            pltpu.SemaphoreType.DMA((count, 2)),
        ],
        compiler_params=pltpu.CompilerParams(
            dimension_semantics=("arbitrary",), vmem_limit_bytes=ATTENTION_MIB * MIB
        ),
        cost_estimate=pl.CostEstimate(
            flops=count * 14 * 10**9, bytes_accessed=count * 8 * MIB, transcendentals=count * 10**6
        ),
    )(start, masks, *halo, qkv, grad_out, w_qkv, *[a for _, a in before], *after)


def on_chip(kernel, out_shape, operands, after=(), scratch=(), flops=10**5, place=()):
    count = len(operands) + len(place)

    def run(*refs):
        kernel(*refs[:count], *refs[count + len(after) :])

    return pl.pallas_call(
        run,
        in_specs=[pl.BlockSpec(memory_space=pltpu.SMEM)] * len(place)
        + [pl.BlockSpec(memory_space=pltpu.VMEM)] * len(operands)
        + [pl.BlockSpec(memory_space=pl.ANY)] * len(after),
        out_specs=[pl.BlockSpec(memory_space=pltpu.VMEM)] * len(out_shape),
        out_shape=[jax.ShapeDtypeStruct(s, d) for s, d in out_shape],
        scratch_shapes=list(scratch),
        compiler_params=pltpu.CompilerParams(vmem_limit_bytes=24 * MIB),
        cost_estimate=pl.CostEstimate(flops=flops, bytes_accessed=10**4, transcendentals=0),
    )(*place, *operands, *after)


def lanes_of(width):
    return [(i, slice(i * LANES, (i + 1) * LANES)) for i in range(width // LANES)]


def project(own, w_qkv, after):
    tokens, width = own.shape
    columns = w_qkv.shape[1]
    block = 4 * LANES

    def kernel(own_ref, w_ref, *refs):
        refs[-1][...] = dot(own_ref[...], w_ref[...]).astype(BF)

    return pl.pallas_call(
        kernel,
        grid=(columns // block,),
        in_specs=[
            pl.BlockSpec((tokens, width), lambda g: (0, 0)),
            pl.BlockSpec((width, block), lambda g: (0, g)),
        ]
        + [pl.BlockSpec(memory_space=pl.ANY)] * len(after),
        out_specs=pl.BlockSpec((tokens, block), lambda g: (0, g)),
        out_shape=jax.ShapeDtypeStruct((tokens, columns), BF),
        compiler_params=pltpu.CompilerParams(vmem_limit_bytes=24 * MIB),
        cost_estimate=pl.CostEstimate(flops=10**9, bytes_accessed=MIB, transcendentals=0),
    )(own, w_qkv, *after)


def input_grads(dq, dkv_1, dkv_2, w_qkv, after):
    tokens, width = dq.shape
    half = width // 2
    pieces = [(0, 0), (0, 1), (1, 0), (2, 0), (1, 1), (2, 1)]

    def kernel(*refs):
        w_ref, out_ref, acc_ref = refs[3], refs[-2], refs[-1]
        for step, (array, part) in enumerate(pieces):

            @pl.when(pl.program_id(0) == step)
            def _():
                product = dot(refs[array][:, part * half : (part + 1) * half], w_ref[...], NT)
                if step == 0:
                    acc_ref[...] = product
                elif step < len(pieces) - 1:
                    acc_ref[...] += product
                else:
                    out_ref[...] = (acc_ref[...] + product).astype(BF)

    whole = pl.BlockSpec((tokens, width), lambda g: (0, 0))
    return pl.pallas_call(
        kernel,
        grid=(len(pieces),),
        in_specs=[whole, whole, whole, pl.BlockSpec((width, half), lambda g: (0, g))]
        + [pl.BlockSpec(memory_space=pl.ANY)] * len(after),
        out_specs=whole,
        out_shape=jax.ShapeDtypeStruct((tokens, width), BF),
        scratch_shapes=[pltpu.VMEM((tokens, width), F32)],
        compiler_params=pltpu.CompilerParams(vmem_limit_bytes=24 * MIB),
        cost_estimate=pl.CostEstimate(flops=4 * 10**9, bytes_accessed=MIB, transcendentals=0),
    )(dq, dkv_1, dkv_2, w_qkv, *after)


def row_blocks(place, own, orders, after):
    tokens, width = own.shape
    devices = len(orders[0])
    size = width // devices
    step = max(1, 16 // size)

    def kernel(place_ref, own_ref, low_ref, high_ref, wide_ref):
        for at in range(0, width, 2 * LANES):
            wide_ref[at : at + 2 * LANES, :] = own_ref[:, at : at + 2 * LANES].astype(F32).T
        even = place_ref[1] == 0
        me = place_ref[2]
        for j in range(0, devices, step):
            rows = []
            for k in range(j, j + step):
                owner = me ^ jnp.where(even, int(orders[0][k]), int(orders[1][k]))
                rows.append(wide_ref[pl.ds(pl.multiple_of(owner * size, size), size), :])
            half, base = divmod(j * size, width // 2)
            block = rows[0] if step == 1 else jnp.concatenate(rows, axis=0)
            (low_ref, high_ref)[half][base : base + step * size, :] = block.astype(BF)

    out = ((width // 2, tokens), BF)
    scratch = [pltpu.VMEM((width, tokens), F32)]
    return on_chip(kernel, [out, out], [own], after=after, scratch=scratch, place=[place])


def pack_sides(own, band_rows, band_cols):
    tokens, width = own.shape

    def kernel(own_ref, last_ref, first_ref, wide_ref):
        for lane, at in lanes_of(width):
            wide_ref[lane] = own_ref[:, at].astype(F32)
            for col in range(MARGIN):
                here = slice(col * band_rows, (col + 1) * band_rows)
                last = pl.ds(band_cols - MARGIN + col, band_rows, stride=band_cols)
                last_ref[here, at] = wide_ref[lane, last, :].astype(BF)
                first = pl.ds(col, band_rows, stride=band_cols)
                first_ref[here, at] = wide_ref[lane, first, :].astype(BF)

    out = ((MARGIN * band_rows, width), BF)
    scratch = [pltpu.VMEM((width // LANES, tokens, LANES), F32)]
    return on_chip(kernel, [out, out], [own], scratch=scratch)


def pack_rows(place, own, band_cols, after):
    tokens, width = own.shape
    edge = MARGIN * band_cols

    def kernel(place_ref, own_ref, out_a, out_b):
        even = place_ref[1] == 0
        last, first = own_ref[tokens - edge :, :], own_ref[:edge, :]
        out_a[...] = jnp.where(even, last, first)
        out_b[...] = jnp.where(even, first, last)

    out = ((edge, width), BF)
    return on_chip(kernel, [out, out], [own], after=after, place=[place])


def pack_corners(place, left, right, band_rows, after):
    width = left.shape[1]

    def kernel(place_ref, left_ref, right_ref, out_a, out_b):
        even = place_ref[1] == 0
        for side, side_ref in enumerate((left_ref, right_ref)):
            for col in range(0, MARGIN, 2):
                base = (side * MARGIN + col) * EDGE_R
                last, first = (
                    jnp.concatenate(
                        [
                            side_ref[at : at + EDGE_R, :].astype(F32)
                            for at in (start, start + band_rows)
                        ]
                    )
                    for start in ((col + 1) * band_rows - EDGE_R, col * band_rows)
                )
                here = slice(base, base + 2 * EDGE_R)
                out_a[here, :] = jnp.where(even, last, first).astype(BF)
                out_b[here, :] = jnp.where(even, first, last).astype(BF)

    out = ((2 * MARGIN * EDGE_R, width), BF)
    return on_chip(kernel, [out, out], [left, right], after=after, place=[place])


def merge_sides(place, left, right, rim_a, rim_b, band_rows, band_cols, after=()):
    edge = MARGIN * band_cols

    def kernel(place_ref, left_ref, right_ref, a_ref, b_ref, ol_ref, or_ref):
        even = place_ref[1] == 0
        for part in range(2):
            for col in range(2 * MARGIN):
                source, target = (left_ref, ol_ref) if col < MARGIN else (right_ref, or_ref)
                base = (col % MARGIN) * band_rows
                pair = slice(edge + (col // 2) * 2 * EDGE_R, edge + (col // 2 + 1) * 2 * EDGE_R)
                odd = slice((col % 2) * EDGE_R, (col % 2 + 1) * EDGE_R)
                rows = source[part, base : base + band_rows, :].astype(F32)
                rim_a, rim_b = (ref[part, pair, :].astype(F32)[odd] for ref in (a_ref, b_ref))
                first = rows[:EDGE_R] + jnp.where(even, rim_b, rim_a)
                last = rows[band_rows - EDGE_R :] + jnp.where(even, rim_a, rim_b)
                target[part, base : base + band_rows, :] = jnp.concatenate(
                    [first, rows[EDGE_R : band_rows - EDGE_R], last], axis=0
                ).astype(BF)

    out = [(left.shape, BF), (right.shape, BF)]
    return on_chip(kernel, out, [left, right, rim_a, rim_b], after=after, place=[place])


def finish(place, mid, rim_a, rim_b, left, right, band_rows, band_cols, after, flops):
    _, tokens, width = mid.shape
    edge = MARGIN * band_cols

    def kernel(place_ref, mid_ref, a_ref, b_ref, left_ref, right_ref, out_ref, acc_ref):
        even = place_ref[1] == 0
        for part in range(2):
            for block in range(width // (2 * LANES)):
                for lane in range(2):
                    at = slice((2 * block + lane) * LANES, (2 * block + lane + 1) * LANES)
                    acc_ref[lane] = mid_ref[part, :, at].astype(F32)
                    from_a, from_b = (r[part, :edge, at].astype(F32) for r in (a_ref, b_ref))
                    acc_ref[lane, :edge, :] += jnp.where(even, from_b, from_a)
                    acc_ref[lane, tokens - edge :, :] += jnp.where(even, from_a, from_b)
                    for col in range(MARGIN):
                        here = slice(col * band_rows, (col + 1) * band_rows)
                        first = pl.ds(col, band_rows, stride=band_cols)
                        last = pl.ds(band_cols - MARGIN + col, band_rows, stride=band_cols)
                        acc_ref[lane, first, :] += left_ref[part, here, at].astype(F32)
                        acc_ref[lane, last, :] += right_ref[part, here, at].astype(F32)
                both = jnp.concatenate([acc_ref[0], acc_ref[1]], axis=1).astype(BF)
                start = part * width + block * 2 * LANES
                out_ref[:, start : start + 2 * LANES] = both

    out = [((tokens, 2 * width), BF)]
    scratch = [pltpu.VMEM((2, tokens, LANES), F32)]
    operands = [mid, rim_a, rim_b, left, right]
    return on_chip(kernel, out, operands, after, scratch, flops, [place])[0]


def grad_rows(rows, columns, scale, kind, after=()):
    features, count = rows.shape[0], len(columns)
    width = columns[0].shape[1]

    def kernel(rows_ref, *refs):
        for i, columns_ref in enumerate(refs[:count]):
            for start in range(0, width, 2 * LANES):
                part = dot(rows_ref[...], columns_ref[:, start : start + 2 * LANES])
                at = i * width + start
                refs[count][:, at : at + 2 * LANES] = (part * scale).astype(kind)

    return on_chip(kernel, [((features, count * width), kind)], [rows, *columns], after)[0]


def add_split(keep, received, after=()):
    half, columns = keep.shape[0] // 2, keep.shape[1]

    def kernel(keep_ref, received_ref, sums_ref, send_ref):
        sums_ref[...] = keep_ref[:half, :] + received_ref[:half, :].astype(F32)
        send_ref[...] = (keep_ref[half:, :] + received_ref[half:, :].astype(F32)).astype(BF)

    return on_chip(kernel, [((half, columns), F32), ((half, columns), BF)], [keep, received], after)


def add_blocks(place, keep, received, blocks, after):
    rows, columns = keep.shape
    size = rows // blocks

    def kernel(place_ref, keep_ref, received_ref, send_ref):
        me = place_ref[2] & (blocks - 1)
        for b in range(blocks):
            here = slice(b * size, (b + 1) * size)
            send_ref[me ^ b] = (keep_ref[here, :] + received_ref[here, :].astype(F32)).astype(BF)

    out = [((blocks, size, columns), BF)]
    return on_chip(kernel, out, [keep, received], after, place=[place])[0]


def sent_blocks(keep, received, blocks, after):
    rows, columns = keep.shape
    size = rows // blocks

    def kernel(keep_ref, received_ref, sums_ref, *sends):
        sums_ref[0] = keep_ref[:size, :] + received_ref[:size, :].astype(F32)
        for b in range(1, blocks):
            here = slice(b * size, (b + 1) * size)
            sends[b - 1][0] = (keep_ref[here, :] + received_ref[here, :].astype(F32)).astype(BF)

    shape = (1, size, columns)
    out = [(shape, F32)] + [(shape, BF)] * (blocks - 1)
    return on_chip(kernel, out, [keep, received], after)


def gather_sums(groups, places, width, flops):
    flat = [array for group in groups for array in group]

    def kernel(*refs):
        out_ref = refs[-1]
        at = 0
        for group, moves in zip(groups, places):
            mine = refs[at : at + len(group)]
            at += len(group)
            for source, size, target in moves:
                here = slice(source, source + size)
                parts = [ref[i, :, here].astype(F32) for ref in mine for i in range(ref.shape[0])]
                out_ref[:, target : target + size] = functools.reduce(lambda a, b: a + b, parts)

    return on_chip(kernel, [((flat[0].shape[1], width), F32)], flat, flops=flops)[0]


def shifted(array, axis, by, wrap):
    size = lax.axis_size(axis)
    route = [(i, (i + by) % size) for i in range(size) if wrap or 0 <= i + by < size]
    return lax.ppermute(array, axis, route)


def swapped(array_a, array_b, axis):
    size = lax.axis_size(axis)
    pairs = [(i, i + 1) for i in range(size - 1)]
    route = lambda chosen: chosen + [(j, i) for i, j in chosen]
    return [
        lax.ppermute(array, axis, route(pairs[offset::2]))
        for array, offset in ((array_a, 0), (array_b, 1))
    ]


def exchanged(array, axis, flip):
    return lax.ppermute(array, axis, [(i, i ^ flip) for i in range(lax.axis_size(axis))])


def bits_of(axis):
    return [(axis, 1 << b) for b in range((lax.axis_size(axis) - 1).bit_length())]


def reduce_stages():
    first, *lat_bits = bits_of("lat")
    bits = bits_of("dp") + lat_bits
    return first, list(zip(bits, reversed(bits)))


def feature_orders(first, stages):
    n_lon, n_lat = lax.axis_size("lon"), lax.axis_size("lat")
    unit = {"lon": 1, "lat": n_lon, "dp": n_lon * n_lat}
    lower = []
    for kind in range(2):
        order = np.arange(n_lon)
        for stage in reversed(stages):
            axis, bit = stage[kind]
            order = np.concatenate([order, order + unit[axis] * bit])
        lower.append(order)
    flip = unit[first[0]] * first[1]
    return [np.concatenate([lower[kind], lower[1 - kind] ^ flip]) for kind in range(2)]


def exchanged_stage(array, stage):
    n_lat, n_dp = lax.axis_size("lat"), lax.axis_size("dp")
    route = []
    for i in range(n_dp * n_lat):
        axis, bit = stage[i % n_lat % 2]
        route.append((i, i ^ (bit * n_lat if axis == "dp" else bit)))
    return lax.ppermute(array, ("dp", "lat"), route)


def body(inputs, grad_out, w_qkv):
    _, band_rows, band_cols, width = inputs.shape
    n_lat, n_lon, n_dp = lax.axis_size("lat"), lax.axis_size("lon"), lax.axis_size("dp")
    band_start = lax.axis_index("lat") * band_rows
    total_rows = band_rows * n_lat
    tokens = band_rows * band_cols
    slots = HEADS // GROUP // 2
    shape = (band_rows, band_cols, total_rows)
    own = inputs.reshape(tokens, width)
    flat_grad = grad_out.reshape(tokens, width)

    last_cols, first_cols = pack_sides(own, band_rows, band_cols)
    left = shifted(last_cols, "lon", 1, True)
    right = shifted(first_cols, "lon", -1, True)
    me = (lax.axis_index("dp") * n_lat + lax.axis_index("lat")) * n_lon + lax.axis_index("lon")
    start = jnp.stack([band_start, lax.axis_index("lat") % 2, me])
    rim_rows = swapped(*pack_rows(start, own, band_cols, [last_cols]), "lat")

    masks = window_masks(start, band_rows, band_cols, total_rows)
    qkv = project(own, w_qkv, [last_cols])
    first, stages = reduce_stages()
    half = width // 2
    rows_keep, rows_send = row_blocks(start, own, feature_orders(first, stages), [last_cols])
    corners = pack_corners(start, left, right, band_rows, [masks, qkv, rows_keep, rows_send])
    halo = (left, right, *rim_rows, *swapped(*corners, "lat"))
    scale = float(tokens * n_dp * n_lat * n_lon) ** -0.5

    attend = lambda first, count, before, after: attention_grads(
        first, count, slots, start, masks, halo, qkv, flat_grad, w_qkv, shape, before, after
    )

    def return_sides(grads, rims, after):
        to_left, to_right = merge_sides(
            start, grads[4], grads[5], *rims, band_rows, band_cols, after
        )
        from_right = shifted(to_left, "lon", -1, True)
        from_left = shifted(to_right, "lon", 1, True)
        return to_left, from_left, from_right

    one = attend(0, slots, [], [])
    rims_1 = swapped(one[1], one[2], "lat")
    two = attend(slots, 1, [(0, one[0])], [])
    sent, *sides_1 = return_sides(one, rims_1, [two[1]])
    two = attend(slots + 1, 1, list(enumerate(two)), [sent])
    rims_2 = swapped(two[1], two[2], "lat")
    dq = two[0]

    dkv_1 = finish(start, one[3], *rims_1, *sides_1, band_rows, band_cols, [dq], 2 * 10**9)
    sent, *sides_2 = return_sides(two, rims_2, [dkv_1])
    send = grad_rows(rows_send, [dq, dkv_1], scale, BF, after=[sent])
    received = exchanged(send, *first)
    keep = grad_rows(rows_keep, [dq, dkv_1], scale, F32, after=[send])
    keep, send = add_split(keep, received)

    dkv_2 = finish(start, two[3], *rims_2, *sides_2, band_rows, band_cols, [keep], FINISH_FLOPS)
    for stage in stages[:-1]:
        keep, send = add_split(keep, exchanged_stage(send, stage), [dkv_2])
    send_2 = grad_rows(rows_send, [dkv_2], scale, BF, after=[keep])
    received = exchanged_stage(send, stages[-1])
    received_2 = exchanged(send_2, *first)
    keep_2 = grad_rows(rows_keep, [dkv_2], scale, F32, after=[send_2])
    keep_2, send_2 = add_split(keep_2, received_2)
    received_2 = exchanged_stage(send_2, stages[0])
    grad_inputs = input_grads(dq, dkv_1, dkv_2, w_qkv, [send_2])
    keep, *send = sent_blocks(keep, received, n_lon, [grad_inputs])
    group_1 = [keep] + [exchanged(a, "lon", i + 1) for i, a in enumerate(send)]
    group_1 = [gather_sums([group_1], [[(0, 2 * width, 0)]], 2 * width, GATHER_FLOPS)[None]]
    for stage in stages[1:]:
        keep_2, send_2 = add_split(keep_2, received_2, [keep])
        received_2 = exchanged_stage(send_2, stage)
    send_2 = add_blocks(start, keep_2, received_2, n_lon, group_1)
    group_2 = [lax.all_to_all(send_2, "lon", 0, 0, tiled=True)]
    places = [
        [(0, width, 0), (width, half, width), (width + half, half, 2 * width)],
        [(0, half, width + half), (half, half, 2 * width + half)],
    ]
    grad_w = gather_sums([group_1, group_2], places, 3 * width, 10**5)

    return (grad_inputs.reshape(inputs.shape), grad_w)


def solution(mesh):
    in_specs = (P("dp", "lat", "lon", None), P("dp", "lat", "lon", None), P())
    out_specs = (P("dp", "lat", "lon", None), P(("dp", "lat", "lon"), None))
    return jax.shard_map(body, mesh=mesh, in_specs=in_specs, out_specs=out_specs, check_vma=False)
```

profile of v0, /device:TPU:0, one launch (start us, length us, event | category | flops | bytes accessed | tf_op | source)
XLA Modules:
  0.0 158.3 jit_solution(17511464462025772140)
XLA Ops:
  3.4 5.0 %collective-permute-start.1 = (bf16[192,1024]{1,0:T(8,128)(2,1)}, bf16[192,1024]{1,0:T(8,128)(2,1)S(1)}, u32[]{:S(2)}, u32[]{:S(2)}) collective-permute-start(bf16[192,1024]{1,0:T(8,128)(2,1)} %get-tuple-element.45), channel_id=1, source_target_pairs={{0,3},{1,0},{2,1},{3,2},{4,7},{5,4},{6,5},{7,6},{8,11},{9,8},{10,9... | collective-permute-start | bytes 1179656 | tf_op jit(solution)/shard_map/ppermute | solution.py:606
  13.4 4.0 %shard_map.50.refs_3_.refs_1_ = bf16[8,512,128]{2,1,0:T(8,128)(2,1)} custom-call(s32[3]{0:T(128)} %copy-done.7), custom_call_target="tpu_custom_call" | custom-call | flops 10000000 | bytes 2097152 | tf_op jit(solution)/shard_map/pallas_call | solution.py:70
  17.4 2.8 %copy-done.4 = bf16[1024,3072]{1,0:T(8,128)(2,1)S(1)} copy-done((bf16[1024,3072]{1,0:T(8,128)(2,1)S(1)}, bf16[1024,3072]{1,0:T(8,128)(2,1)}, u32[]{:S(2)}) %copy-start.4) | copy-done | bytes 6291480
  20.2 4.9 %shard_map.53.refs_4_.refs_8_ = bf16[512,3072]{1,0:T(8,128)(2,1)S(1)} custom-call(bf16[512,1024]{1,0:T(8,128)(2,1)S(1)} %bitcast.10, bf16[1024,3072]{1,0:T(8,128)(2,1)S(1)} %copy-done.4, bf16[192,1024]{1,0:T(8,128)(2,1)S(1)} %get-tuple-element.44.refs_2_.refs_0_), custom_call_target="tpu_custom_call" | custom-call | flops 1000000000 | bytes 1048576 | tf_op jit(solution)/shard_map/pallas_call | solution.py:350
  27.0 2.0 %collective-permute-start.4 = (bf16[96,1024]{1,0:T(8,128)(2,1)S(1)}, bf16[96,1024]{1,0:T(8,128)(2,1)S(1)}, u32[]{:S(2)}, u32[]{:S(2)}) collective-permute-start(bf16[96,1024]{1,0:T(8,128)(2,1)S(1)} %get-tuple-element.50), channel_id=1, source_target_pairs={{0,4},{8,12},{4,0},{12,8},{1,5},{9,13},{5,1},{13,9},{2,6},{10,14},... | collective-permute-start | bytes 589832 | tf_op jit(solution)/shard_map/ppermute | solution.py:614
  30.0 19.7 %shard_map.56 = (bf16[512,1024]{1,0:T(8,128)(2,1)S(1)}, bf16[2,192,512]{2,1,0:T(8,128)(2,1)S(1)}, bf16[2,192,512]{2,1,0:T(8,128)(2,1)S(1)}, bf16[2,512,512]{2,1,...) custom-call(s32[3]{0:T(128)S(1)} %copy-done.8, ...), custom_call_target="tpu_custom_call" | custom-call | flops 28000000000 | bytes 16777216 | tf_op jit(solution)/shard_map/pallas_call | solution.py:280
  49.7 6.0 %collective-permute-start.6 = (bf16[2,192,512]{2,1,0:T(8,128)(2,1)S(1)}, bf16[2,192,512]{2,1,0:T(8,128)(2,1)S(1)}, u32[]{:S(2)}, u32[]{:S(2)}) collective-permute-start(bf16[2,192,512]{2,1,0:T(8,128)(2,1)S(1)} %get-tuple-element.61), channel_id=1, source_target_pairs={{0,4},{8,12},{4,0},{12,8},{1,5},{9,13},{5,1},{13,9},{2,6},{10,14},... | collective-permute-start | bytes 1179656 | tf_op jit(solution)/shard_map/ppermute | solution.py:614
  56.6 10.9 %shard_map.57 = (bf16[512,1024]{1,0:T(8,128)(2,1)S(1)}, bf16[2,192,512]{2,1,0:T(8,128)(2,1)S(1)}, bf16[2,192,512]{2,1,0:T(8,128)(2,1)S(1)}, bf16[2,512,512]{2,1,...) custom-call(s32[3]{0:T(128)S(1)} %copy-done.8, ...), custom_call_target="tpu_custom_call", output_to_operand_aliasing={{0}: (11, {})} | custom-call | flops 14000000000 | bytes 8388608 | tf_op jit(solution)/shard_map/pallas_call | solution.py:280
  68.4 3.7 %collective-permute-start.9 = (bf16[2,192,512]{2,1,0:T(8,128)(2,1)S(1)}, bf16[2,192,512]{2,1,0:T(8,128)(2,1)S(1)}, u32[]{:S(2)}, u32[]{:S(2)}) collective-permute-start(bf16[2,192,512]{2,1,0:T(8,128)(2,1)S(1)} %get-tuple-element.63.refs_17_), channel_id=1, source_target_pairs={{0,3},{1,0},{2,1},{3,2},{4,7},{5,4},{6,5},{7,6},{8,11},{9,8},{10,9... | collective-permute-start | bytes 1179656 | tf_op jit(solution)/shard_map/ppermute | solution.py:606
  72.1 10.9 %shard_map.59 = (bf16[512,1024]{1,0:T(8,128)(2,1)S(1)}, bf16[2,192,512]{2,1,0:T(8,128)(2,1)S(1)}, bf16[2,192,512]{2,1,0:T(8,128)(2,1)S(1)}, bf16[2,512,512]{2,1,...) custom-call(s32[3]{0:T(128)S(1)} %copy-done.8, ...), custom_call_target="tpu_custom_call", output_to_operand_aliasing={{0}: (11, {}), {1}: (12, {}), {2}: (13, {}), {3}: (14, {}),... | custom-call | flops 14000000000 | bytes 8388608 | tf_op jit(solution)/shard_map/pallas_call | solution.py:280
  85.5 2.2 %collective-permute-done.9.refs_5_ = bf16[2,192,512]{2,1,0:T(8,128)(2,1)S(1)} collective-permute-done((bf16[2,192,512]{2,1,0:T(8,128)(2,1)S(1)}, bf16[2,192,512]{2,1,0:T(8,128)(2,1)S(1)}, u32[]{:S(2)}, u32[]{:S(2)}) %collective-permute-start.9) | collective-permute-done | bytes 393248 | tf_op jit(solution)/shard_map/ppermute | solution.py:606
  87.7 1.9 %shard_map.60.refs_5_.refs_2_.refs_1_ = bf16[512,1024]{1,0:T(8,128)(2,1)S(1)} custom-call(s32[3]{0:T(128)S(1)} %copy-done.8, bf16[2,512,512]{2,1,0:T(8,128)(2,1)S(1)} %get-tuple-element.65.refs_1_, bf16[2,192,512]{2,1,0:T(8,128)(2,1)S(1)} %collective-permute-done.6.refs_3_.refs_2_, bf16[2,192,512]{2,1,0:T(8,128)(2,1)S(1)} %collective-permute-done.7.refs_4_.refs_3_, ...), custom_call_target="tpu_custom_call" | custom-call | flops 2000000000 | bytes 10000 | tf_op jit(solution)/shard_map/pallas_call | solution.py:325
  91.6 4.1 %collective-permute-start.14 = (bf16[512,2048]{1,0:T(8,128)(2,1)S(1)}, bf16[512,2048]{1,0:T(8,128)(2,1)S(1)}, u32[]{:S(2)}, u32[]{:S(2)}) collective-permute-start(bf16[512,2048]{1,0:T(8,128)(2,1)S(1)} %shard_map.62.refs_3_), channel_id=1, source_target_pairs={{0,4},{4,0},{8,12},{12,8},{1,5},{5,1},{9,13},{13,9},{2,6},{6,2},{1... | collective-permute-start | bytes 6291464 | tf_op jit(solution)/shard_map/ppermute | solution.py:620
  95.7 3.8 %collective-permute-start.13 = (bf16[2,192,512]{2,1,0:T(8,128)(2,1)S(1)}, bf16[2,192,512]{2,1,0:T(8,128)(2,1)S(1)}, u32[]{:S(2)}, u32[]{:S(2)}) collective-permute-start(bf16[2,192,512]{2,1,0:T(8,128)(2,1)S(1)} %get-tuple-element.73.refs_3_), channel_id=1, source_target_pairs={{0,3},{1,0},{2,1},{3,2},{4,7},{5,4},{6,5},{7,6},{8,11},{9,8},{10,9... | collective-permute-start | bytes 1179656 | tf_op jit(solution)/shard_map/ppermute | solution.py:606
  102.7 6.8 %collective-permute-done.12.refs_4_ = bf16[2,192,512]{2,1,0:T(8,128)(2,1)S(1)} collective-permute-done((bf16[2,192,512]{2,1,0:T(8,128)(2,1)S(1)}, bf16[2,192,512]{2,1,0:T(8,128)(2,1)S(1)}, u32[]{:S(2)}, u32[]{:S(2)}) %collective-permute-start.12) | collective-permute-done | bytes 393248 | tf_op jit(solution)/shard_map/ppermute | solution.py:606
  109.5 5.8 %collective-permute-done.13.refs_5_ = bf16[2,192,512]{2,1,0:T(8,128)(2,1)S(1)} collective-permute-done((bf16[2,192,512]{2,1,0:T(8,128)(2,1)S(1)}, bf16[2,192,512]{2,1,0:T(8,128)(2,1)S(1)}, u32[]{:S(2)}, u32[]{:S(2)}) %collective-permute-start.13) | collective-permute-done | bytes 393248 | tf_op jit(solution)/shard_map/ppermute | solution.py:606
  115.3 1.9 %shard_map.65.refs_2_.refs_1_ = bf16[512,1024]{1,0:T(8,128)(2,1)S(1)} custom-call(s32[3]{0:T(128)S(1)} %copy-done.8, bf16[2,512,512]{2,1,0:T(8,128)(2,1)S(1)} %get-tuple-element.67.refs_1_, bf16[2,192,512]{2,1,0:T(8,128)(2,1)S(1)} %collective-permute-done.10.refs_3_.refs_2_, bf16[2,192,512]{2,1,0:T(8,128)(2,1)S(1)} %collective-permute-done.11.refs_4_.refs_3_, ...), custom_call_target="tpu_custom_call" | custom-call | flops 8999999488 | bytes 10000 | tf_op jit(solution)/shard_map/pallas_call | solution.py:325
  118.3 1.7 %collective-permute-start.17 = (bf16[128,2048]{1,0:T(8,128)(2,1)S(1)}, bf16[128,2048]{1,0:T(8,128)(2,1)S(1)}, u32[]{:S(2)}, u32[]{:S(2)}) collective-permute-start(bf16[128,2048]{1,0:T(8,128)(2,1)S(1)} %get-tuple-element.78), channel_id=1, source_target_pairs={{0,8},{4,20},{8,0},{12,28},{16,24},{20,4},{24,16},{28,12},{1,9},{5... | collective-permute-start | bytes 1572872 | tf_op jit(solution)/shard_map/ppermute | solution.py:653
  122.6 6.1 %shard_map.70.refs_2_ = bf16[512,1024]{1,0:T(8,128)(2,1)} custom-call(bf16[512,1024]{1,0:T(8,128)(2,1)S(1)} %get-tuple-element.64.refs_6_.refs_1_.refs_0_, bf16[512,1024]{1,0:T(8,128)(2,1)S(1)} %shard_map.60.refs_5_.refs_2_.refs_1_, bf16[512,1024]{1,0:T(8,128)(2,1)S(1)} %shard_map.65.refs_2_.refs_1_, bf16[1024,3072]{1,0:T(8,128)(2,1)S(1)} %bitcast.12, ...), custom_call_target="tpu_custom_call" | custom-call | flops 4000000000 | bytes 1048576 | tf_op jit(solution)/shard_map/pallas_call | solution.py:385
  128.7 2.4 %collective-permute-done.17.refs_1_ = bf16[128,2048]{1,0:T(8,128)(2,1)S(1)} collective-permute-done((bf16[128,2048]{1,0:T(8,128)(2,1)S(1)}, bf16[128,2048]{1,0:T(8,128)(2,1)S(1)}, u32[]{:S(2)}, u32[]{:S(2)}) %collective-permute-start.17) | collective-permute-done | bytes 524320 | tf_op jit(solution)/shard_map/ppermute | solution.py:653
  132.9 2.1 %collective-permute-start.19 = (bf16[1,32,2048]{2,1,0:T(8,128)(2,1)S(1)}, bf16[1,32,2048]{2,1,0:T(8,128)(2,1)S(1)}, u32[]{:S(2)}, u32[]{:S(2)}) collective-permute-start(bf16[1,32,2048]{2,1,0:T(8,128)(2,1)S(1)} %get-tuple-element.81), channel_id=1, source_target_pairs={{0,2},{1,3},{2,0},{3,1},{4,6},{5,7},{6,4},{7,5},{8,10},{9,11},{10,... | collective-permute-start | bytes 393224 | tf_op jit(solution)/shard_map/ppermute | solution.py:620
  135.1 1.8 %collective-permute-start.20 = (bf16[1,32,2048]{2,1,0:T(8,128)(2,1)S(1)}, bf16[1,32,2048]{2,1,0:T(8,128)(2,1)S(1)}, u32[]{:S(2)}, u32[]{:S(2)}) collective-permute-start(bf16[1,32,2048]{2,1,0:T(8,128)(2,1)S(1)} %get-tuple-element.82), channel_id=1, source_target_pairs={{0,3},{1,2},{2,1},{3,0},{4,7},{5,6},{6,5},{7,4},{8,11},{9,10},{10,... | collective-permute-start | bytes 393224 | tf_op jit(solution)/shard_map/ppermute | solution.py:620
  138.7 6.2 %collective-permute-done.19.refs_2_ = bf16[1,32,2048]{2,1,0:T(8,128)(2,1)S(1)} collective-permute-done((bf16[1,32,2048]{2,1,0:T(8,128)(2,1)S(1)}, bf16[1,32,2048]{2,1,0:T(8,128)(2,1)S(1)}, u32[]{:S(2)}, u32[]{:S(2)}) %collective-permute-start.19) | collective-permute-done | bytes 131104 | tf_op jit(solution)/shard_map/ppermute | solution.py:620
  145.5 11.9 %all_to_all.5.refs_1_ = bf16[4,32,1024]{2,1,0:T(8,128)(2,1)S(1)} all-to-all(bf16[4,32,1024]{2,1,0:T(8,128)(2,1)S(1)} %shard_map.74), channel_id=1, replica_groups=mesh['dp'=2,'lat'=4,'lon'=4] {'lon'}, dimensions={0} | all-to-all | bytes 524288 | tf_op jit(solution)/shard_map/all_to_all | solution.py:727
  (75 shorter events, 28.7 us)
Async XLA Ops:
  1.9 15.6 %copy-start.2 = (bf16[1,32,16,1024]{3,2,1,0:T(8,128)(2,1)S(1)}, bf16[1,32,16,1024]{3,2,1,0:T(8,128)(2,1)}, u32[]{:S(2)}) copy-start(bf16[1,32,16,1024]{3,2,1,0:T(8,128)(2,1)} %param.3) | copy-start | bytes 3145732
  3.4 21.7 %collective-permute-start.1 = (bf16[192,1024]{1,0:T(8,128)(2,1)}, bf16[192,1024]{1,0:T(8,128)(2,1)S(1)}, u32[]{:S(2)}, u32[]{:S(2)}) collective-permute-start(bf16[192,1024]{1,0:T(8,128)(2,1)} %get-tuple-element.45), channel_id=1, source_target_pairs={{0,3},{1,0},{2,1},{3,2},{4,7},{5,4},{6,5},{7,6},{8,11},{9,8},{10,9... | collective-permute-start | bytes 1179656 | tf_op jit(solution)/shard_map/ppermute | solution.py:606
  8.4 17.9 %collective-permute-start = (bf16[192,1024]{1,0:T(8,128)(2,1)S(1)}, bf16[192,1024]{1,0:T(8,128)(2,1)S(1)}, u32[]{:S(2)}, u32[]{:S(2)}) collective-permute-start(bf16[192,1024]{1,0:T(8,128)(2,1)S(1)} %get-tuple-element.44.refs_2_.refs_0_), channel_id=1, source_target_pairs={{0,1},{1,2},{2,3},{3,0},{4,5},{5,6},{6,7},{7,4},{8,9},{9,10},{10,1... | collective-permute-start | bytes 1179656 | tf_op jit(solution)/shard_map/ppermute | solution.py:606
  11.0 18.6 %collective-permute-start.2 = (bf16[96,1024]{1,0:T(8,128)(2,1)}, bf16[96,1024]{1,0:T(8,128)(2,1)S(1)}, u32[]{:S(2)}, u32[]{:S(2)}) collective-permute-start(bf16[96,1024]{1,0:T(8,128)(2,1)} %get-tuple-element.46), channel_id=1, source_target_pairs={{0,4},{8,12},{4,0},{12,8},{1,5},{9,13},{5,1},{13,9},{2,6},{10,14},... | collective-permute-start | bytes 589832 | tf_op jit(solution)/shard_map/ppermute | solution.py:614
  11.0 18.6 %collective-permute-start.3 = (bf16[96,1024]{1,0:T(8,128)(2,1)}, bf16[96,1024]{1,0:T(8,128)(2,1)}, u32[]{:S(2)}, u32[]{:S(2)}) collective-permute-start(bf16[96,1024]{1,0:T(8,128)(2,1)} %get-tuple-element.47), channel_id=1, source_target_pairs={{4,8},{8,4},{5,9},{9,5},{6,10},{10,6},{7,11},{11,7},{20,24},{24,20... | collective-permute-start | bytes 589832 | tf_op jit(solution)/shard_map/ppermute | solution.py:614
  27.0 3.0 %collective-permute-start.4 = (bf16[96,1024]{1,0:T(8,128)(2,1)S(1)}, bf16[96,1024]{1,0:T(8,128)(2,1)S(1)}, u32[]{:S(2)}, u32[]{:S(2)}) collective-permute-start(bf16[96,1024]{1,0:T(8,128)(2,1)S(1)} %get-tuple-element.50), channel_id=1, source_target_pairs={{0,4},{8,12},{4,0},{12,8},{1,5},{9,13},{5,1},{13,9},{2,6},{10,14},... | collective-permute-start | bytes 589832 | tf_op jit(solution)/shard_map/ppermute | solution.py:614
  28.9 1.1 collective-permute-start.5
  49.7 17.7 %collective-permute-start.6 = (bf16[2,192,512]{2,1,0:T(8,128)(2,1)S(1)}, bf16[2,192,512]{2,1,0:T(8,128)(2,1)S(1)}, u32[]{:S(2)}, u32[]{:S(2)}) collective-permute-start(bf16[2,192,512]{2,1,0:T(8,128)(2,1)S(1)} %get-tuple-element.61), channel_id=1, source_target_pairs={{0,4},{8,12},{4,0},{12,8},{1,5},{9,13},{5,1},{13,9},{2,6},{10,14},... | collective-permute-start | bytes 1179656 | tf_op jit(solution)/shard_map/ppermute | solution.py:614
  55.7 11.8 %collective-permute-start.7 = (bf16[2,192,512]{2,1,0:T(8,128)(2,1)S(1)}, bf16[2,192,512]{2,1,0:T(8,128)(2,1)S(1)}, u32[]{:S(2)}, u32[]{:S(2)}) collective-permute-start(bf16[2,192,512]{2,1,0:T(8,128)(2,1)S(1)} %get-tuple-element.62), channel_id=1, source_target_pairs={{4,8},{8,4},{5,9},{9,5},{6,10},{10,6},{7,11},{11,7},{20,24},{24,20... | collective-permute-start | bytes 1179656 | tf_op jit(solution)/shard_map/ppermute | solution.py:614
  68.2 17.4 %collective-permute-start.8 = (bf16[2,192,512]{2,1,0:T(8,128)(2,1)S(1)}, bf16[2,192,512]{2,1,0:T(8,128)(2,1)S(1)}, u32[]{:S(2)}, u32[]{:S(2)}) collective-permute-start(bf16[2,192,512]{2,1,0:T(8,128)(2,1)S(1)} %get-tuple-element.66), channel_id=1, source_target_pairs={{0,1},{1,2},{2,3},{3,0},{4,5},{5,6},{6,7},{7,4},{8,9},{9,10},{10,1... | collective-permute-start | bytes 1179656 | tf_op jit(solution)/shard_map/ppermute | solution.py:606
  68.4 19.3 %collective-permute-start.9 = (bf16[2,192,512]{2,1,0:T(8,128)(2,1)S(1)}, bf16[2,192,512]{2,1,0:T(8,128)(2,1)S(1)}, u32[]{:S(2)}, u32[]{:S(2)}) collective-permute-start(bf16[2,192,512]{2,1,0:T(8,128)(2,1)S(1)} %get-tuple-element.63.refs_17_), channel_id=1, source_target_pairs={{0,3},{1,0},{2,1},{3,2},{4,7},{5,4},{6,5},{7,6},{8,11},{9,8},{10,9... | collective-permute-start | bytes 1179656 | tf_op jit(solution)/shard_map/ppermute | solution.py:606
  83.0 6.7 %collective-permute-start.10 = (bf16[2,192,512]{2,1,0:T(8,128)(2,1)S(1)}, bf16[2,192,512]{2,1,0:T(8,128)(2,1)S(1)}, u32[]{:S(2)}, u32[]{:S(2)}) collective-permute-start(bf16[2,192,512]{2,1,0:T(8,128)(2,1)S(1)} %get-tuple-element.68), channel_id=1, source_target_pairs={{0,4},{8,12},{4,0},{12,8},{1,5},{9,13},{5,1},{13,9},{2,6},{10,14},... | collective-permute-start | bytes 1179656 | tf_op jit(solution)/shard_map/ppermute | solution.py:614
  84.6 5.0 %collective-permute-start.11 = (bf16[2,192,512]{2,1,0:T(8,128)(2,1)S(1)}, bf16[2,192,512]{2,1,0:T(8,128)(2,1)S(1)}, u32[]{:S(2)}, u32[]{:S(2)}) collective-permute-start(bf16[2,192,512]{2,1,0:T(8,128)(2,1)S(1)} %get-tuple-element.69), channel_id=1, source_target_pairs={{4,8},{8,4},{5,9},{9,5},{6,10},{10,6},{7,11},{11,7},{20,24},{24,20... | collective-permute-start | bytes 1179656 | tf_op jit(solution)/shard_map/ppermute | solution.py:614
  91.6 9.2 %collective-permute-start.14 = (bf16[512,2048]{1,0:T(8,128)(2,1)S(1)}, bf16[512,2048]{1,0:T(8,128)(2,1)S(1)}, u32[]{:S(2)}, u32[]{:S(2)}) collective-permute-start(bf16[512,2048]{1,0:T(8,128)(2,1)S(1)} %shard_map.62.refs_3_), channel_id=1, source_target_pairs={{0,4},{4,0},{8,12},{12,8},{1,5},{5,1},{9,13},{13,9},{2,6},{6,2},{1... | collective-permute-start | bytes 6291464 | tf_op jit(solution)/shard_map/ppermute | solution.py:620
  95.7 13.8 %collective-permute-start.12 = (bf16[2,192,512]{2,1,0:T(8,128)(2,1)S(1)}, bf16[2,192,512]{2,1,0:T(8,128)(2,1)S(1)}, u32[]{:S(2)}, u32[]{:S(2)}) collective-permute-start(bf16[2,192,512]{2,1,0:T(8,128)(2,1)S(1)} %get-tuple-element.72), channel_id=1, source_target_pairs={{0,1},{1,2},{2,3},{3,0},{4,5},{5,6},{6,7},{7,4},{8,9},{9,10},{10,1... | collective-permute-start | bytes 1179656 | tf_op jit(solution)/shard_map/ppermute | solution.py:606
  95.7 19.6 %collective-permute-start.13 = (bf16[2,192,512]{2,1,0:T(8,128)(2,1)S(1)}, bf16[2,192,512]{2,1,0:T(8,128)(2,1)S(1)}, u32[]{:S(2)}, u32[]{:S(2)}) collective-permute-start(bf16[2,192,512]{2,1,0:T(8,128)(2,1)S(1)} %get-tuple-element.73.refs_3_), channel_id=1, source_target_pairs={{0,3},{1,0},{2,1},{3,2},{4,7},{5,4},{6,5},{7,6},{8,11},{9,8},{10,9... | collective-permute-start | bytes 1179656 | tf_op jit(solution)/shard_map/ppermute | solution.py:606
  101.2 16.1 %collective-permute-start.15 = (bf16[256,2048]{1,0:T(8,128)(2,1)S(1)}, bf16[256,2048]{1,0:T(8,128)(2,1)S(1)}, u32[]{:S(2)}, u32[]{:S(2)}) collective-permute-start(bf16[256,2048]{1,0:T(8,128)(2,1)S(1)} %get-tuple-element.75), channel_id=1, source_target_pairs={{0,16},{4,12},{8,24},{12,4},{16,0},{20,28},{24,8},{28,20},{1,17},{... | collective-permute-start | bytes 3145736 | tf_op jit(solution)/shard_map/ppermute | solution.py:653
  118.2 2.7 %collective-permute-start.16 = (bf16[512,1024]{1,0:T(8,128)(2,1)S(1)}, bf16[512,1024]{1,0:T(8,128)(2,1)S(1)}, u32[]{:S(2)}, u32[]{:S(2)}) collective-permute-start(bf16[512,1024]{1,0:T(8,128)(2,1)S(1)} %shard_map.67.refs_2_), channel_id=1, source_target_pairs={{0,4},{4,0},{8,12},{12,8},{1,5},{5,1},{9,13},{13,9},{2,6},{6,2},{1... | collective-permute-start | bytes 3145736 | tf_op jit(solution)/shard_map/ppermute | solution.py:620
  118.3 12.8 %collective-permute-start.17 = (bf16[128,2048]{1,0:T(8,128)(2,1)S(1)}, bf16[128,2048]{1,0:T(8,128)(2,1)S(1)}, u32[]{:S(2)}, u32[]{:S(2)}) collective-permute-start(bf16[128,2048]{1,0:T(8,128)(2,1)S(1)} %get-tuple-element.78), channel_id=1, source_target_pairs={{0,8},{4,20},{8,0},{12,28},{16,24},{20,4},{24,16},{28,12},{1,9},{5... | collective-permute-start | bytes 1572872 | tf_op jit(solution)/shard_map/ppermute | solution.py:653
  121.1 15.8 %collective-permute-start.21 = (bf16[256,1024]{1,0:T(8,128)(2,1)S(1)}, bf16[256,1024]{1,0:T(8,128)(2,1)S(1)}, u32[]{:S(2)}, u32[]{:S(2)}) collective-permute-start(bf16[256,1024]{1,0:T(8,128)(2,1)S(1)} %get-tuple-element.77.refs_4_), channel_id=1, source_target_pairs={{0,16},{4,12},{8,24},{12,4},{16,0},{20,28},{24,8},{28,20},{1,17},{... | collective-permute-start | bytes 1572872 | tf_op jit(solution)/shard_map/ppermute | solution.py:653
  132.4 6.3 %collective-permute-start.18 = (bf16[1,32,2048]{2,1,0:T(8,128)(2,1)S(1)}, bf16[1,32,2048]{2,1,0:T(8,128)(2,1)S(1)}, u32[]{:S(2)}, u32[]{:S(2)}) collective-permute-start(bf16[1,32,2048]{2,1,0:T(8,128)(2,1)S(1)} %get-tuple-element.80), channel_id=1, source_target_pairs={{0,1},{1,0},{2,3},{3,2},{4,5},{5,4},{6,7},{7,6},{8,9},{9,8},{10,11... | collective-permute-start | bytes 393224 | tf_op jit(solution)/shard_map/ppermute | solution.py:620
  132.9 11.9 %collective-permute-start.19 = (bf16[1,32,2048]{2,1,0:T(8,128)(2,1)S(1)}, bf16[1,32,2048]{2,1,0:T(8,128)(2,1)S(1)}, u32[]{:S(2)}, u32[]{:S(2)}) collective-permute-start(bf16[1,32,2048]{2,1,0:T(8,128)(2,1)S(1)} %get-tuple-element.81), channel_id=1, source_target_pairs={{0,2},{1,3},{2,0},{3,1},{4,6},{5,7},{6,4},{7,5},{8,10},{9,11},{10,... | collective-permute-start | bytes 393224 | tf_op jit(solution)/shard_map/ppermute | solution.py:620
  135.1 9.8 %collective-permute-start.20 = (bf16[1,32,2048]{2,1,0:T(8,128)(2,1)S(1)}, bf16[1,32,2048]{2,1,0:T(8,128)(2,1)S(1)}, u32[]{:S(2)}, u32[]{:S(2)}) collective-permute-start(bf16[1,32,2048]{2,1,0:T(8,128)(2,1)S(1)} %get-tuple-element.82), channel_id=1, source_target_pairs={{0,3},{1,2},{2,1},{3,0},{4,7},{5,6},{6,5},{7,4},{8,11},{9,10},{10,... | collective-permute-start | bytes 393224 | tf_op jit(solution)/shard_map/ppermute | solution.py:620
  137.0 8.0 %collective-permute-start.22 = (bf16[128,1024]{1,0:T(8,128)(2,1)S(1)}, bf16[128,1024]{1,0:T(8,128)(2,1)S(1)}, u32[]{:S(2)}, u32[]{:S(2)}) collective-permute-start(bf16[128,1024]{1,0:T(8,128)(2,1)S(1)} %get-tuple-element.85), channel_id=1, source_target_pairs={{0,8},{4,20},{8,0},{12,28},{16,24},{20,4},{24,16},{28,12},{1,9},{5... | collective-permute-start | bytes 786440 | tf_op jit(solution)/shard_map/ppermute | solution.py:653
  (11 other events, 37.5 us)
where the time goes:
time: 159 us; the launch traced here: 158 us
  Pallas kernels  72.3 us (45%)
  starting transfers between devices  41.4 us (26%)
  waiting for transfers between devices  25.1 us (16%)
  blocking collectives  11.9 us (7%)
  local copies, waits for them, and re-layouts  6.49 us (4%)
    pallas_call x3, Pallas kernels, attention_grads(): pl.pallas_call(functools.partial(attention_kernel, band_rows, band_cols,...  41.5 us
    ppermute x6, waiting for transfers between devices, shifted(): return lax.ppermute(array, axis, route)  16 us
    pallas_call x20, Pallas kernels, on_chip(): pl.pallas_call(run, in_specs=[pl.BlockSpec(memory_space=pltpu.SMEM)] * le...  15.9 us
    ppermute x8, starting transfers between devices, swapped(): lax.ppermute(array, axis, route(pairs[offset::2]))  13.3 us
    ppermute x6, starting transfers between devices, shifted(): return lax.ppermute(array, axis, route)  12.8 us
    all_to_all x1, blocking collectives, body(): group_2 = [lax.all_to_all(send_2, 'lon', 0, 0, tiled=True)]  11.9 us
    ppermute x5, starting transfers between devices, exchanged(): lax.ppermute(array, axis, [(i, i ^ flip) for i in range(lax.axis_size(axi...  8.65 us
    ppermute x4, starting transfers between devices, exchanged_stage(): return lax.ppermute(array, ('dp', 'lat'), route)  6.62 us
  transfers between devices with their start and end apart: 23, of which 8 were waited for; matrix products, arithmetic and copies ran while one was open for 0% of the time, Pallas kernels for 29%

commit v1 on v0

--- a/solution.py
+++ b/solution.py
@@ -77,10 +77,11 @@
     )(start)
 
 
-def attention_kernel(band_rows, band_cols, total_rows, head_width, extra, first, count, *refs):
+def attention_kernel(band_rows, band_cols, total_rows, head_width, extra, first, count, shift, *refs):
     (place_ref, mask_ref, left_ref, right_ref, rows_a, rows_b, corners_a, corners_b,
      qkv_hbm, grad_hbm, w_hbm) = refs[:11]
-    (dq_ref, out_a, out_b, mid_ref, to_left_ref, to_right_ref,
+    before_a, before_b = refs[11 : 11 + shift], refs[11 + shift : 11 + 2 * shift]
+    (dq_all, out_a_all, out_b_all, mid_all, to_left_all, to_right_all,
      halo_ref, spot_ref, q_ref, k_ref, v_ref, dk_ref, dv_ref,
      own_refs, w_refs, own_sem, w_sem) = refs[11 + extra :]
     band_start = place_ref[0]
@@ -101,6 +102,10 @@
     halves = [(i, slice(i * LANES, (i + 1) * LANES)) for i in range(width // LANES)]
 
     step = pl.program_id(0)
+    dq_ref, mid_ref, to_left_ref, to_right_ref = (
+        ref.at[step] for ref in (dq_all, mid_all, to_left_all, to_right_all)
+    )
+    out_a, out_b = (ref.at[step + shift] for ref in (out_a_all, out_b_all))
     groups = HEADS // GROUP
 
     def copies(slot, parts):
@@ -123,6 +128,9 @@
 
     @pl.when(step == 0)
     def _():
+        for ref, kept in ((out_a_all, before_a), (out_b_all, before_b)):
+            for i in range(shift):
+                ref[i] = kept[0][i]
         for slot in range(count):
             for copy in copies(slot, for_k + for_v + for_q):
                 copy.start()
@@ -254,9 +262,7 @@
                 ].astype(BF)
 
 
-def attention_grads(
-    first, count, slots, start, masks, halo, qkv, grad_out, w_qkv, shape, before, after
-):
+def attention_grads(first, count, place, masks, halo, qkv, grad_out, w_qkv, shape, before, after):
     band_rows, band_cols, total_rows = shape
     tokens, width = grad_out.shape
     head_width = width // HEADS
@@ -267,33 +273,29 @@
     edge = MARGIN * (band_cols + 2 * EDGE_R)
     corner = 2 * MARGIN * EDGE_R
     halo_tokens = 2 * (side + MARGIN * band_cols + corner)
-    whole = lambda g: (0, 0)
-    column = lambda offset: (lambda g: (0, offset + first + g))
-    slot = lambda g: (0, 0, first % slots + g)
-    halves = [(2, edge), (2, edge), (2, tokens), (2, side), (2, side)]
-    out_shape = [jax.ShapeDtypeStruct((tokens, width), BF)] + [
-        jax.ShapeDtypeStruct(s + (slots * block,), BF) for s in halves
+    shift = before[0].shape[0] if before else 0
+    vmem = pl.BlockSpec(memory_space=pltpu.VMEM)
+    shapes = [
+        (count, tokens, block),
+        (count + shift, 2, edge, block),
+        (count + shift, 2, edge, block),
+        (count, 2, tokens, block),
+        (count, 2, side, block),
+        (count, 2, side, block),
     ]
-    aliases = {}
-    if before:
-        aliases = {11 + i: place for i, (place, _) in enumerate(before)}
     return pl.pallas_call(
         functools.partial(
             attention_kernel, band_rows, band_cols, total_rows, head_width,
-            len(before) + len(after), first, count,
+            len(before) + len(after), first, count, shift,
         ),
         grid=(count,),
-        in_specs=[
-            pl.BlockSpec(memory_space=pltpu.SMEM),
-            pl.BlockSpec(masks.shape, lambda g: (0, 0, 0)),
-        ]
-        + [pl.BlockSpec(piece.shape, whole) for piece in halo]
+        in_specs=[pl.BlockSpec(memory_space=pltpu.SMEM)]
+        + [vmem] * (1 + len(halo))
         + [pl.BlockSpec(memory_space=pltpu.HBM)] * 3
-        + [pl.BlockSpec(memory_space=pl.ANY)] * (len(before) + len(after)),
-        out_specs=[pl.BlockSpec((tokens, block), column(0))]
-        + [pl.BlockSpec(s + (block,), slot) for s in halves],
-        out_shape=out_shape,
-        input_output_aliases=aliases,
+        + [vmem] * len(before)
+        + [pl.BlockSpec(memory_space=pl.ANY)] * len(after),
+        out_specs=[vmem] * len(shapes),
+        out_shape=[jax.ShapeDtypeStruct(s, BF) for s in shapes],
         scratch_shapes=[
             pltpu.VMEM((halo_tokens, width), BF),
             pltpu.VMEM((block // LANES, (band_rows + 2 * MARGIN) * HALO_COLS, LANES), F32),
@@ -313,7 +315,7 @@
         cost_estimate=pl.CostEstimate(
             flops=count * 14 * 10**9, bytes_accessed=count * 8 * MIB, transcendentals=count * 10**6
         ),
-    )(start, masks, *halo, qkv, grad_out, w_qkv, *[a for _, a in before], *after)
+    )(place, masks, *halo, qkv, grad_out, w_qkv, *before, *after)
 
 
 def on_chip(kernel, out_shape, operands, after=(), scratch=(), flops=10**5, place=()):
@@ -362,37 +364,47 @@
     )(own, w_qkv, *after)
 
 
-def input_grads(dq, dkv_1, dkv_2, w_qkv, after):
-    tokens, width = dq.shape
-    half = width // 2
-    pieces = [(0, 0), (0, 1), (1, 0), (2, 0), (1, 1), (2, 1)]
+def input_grads(columns, w_qkv, after):
+    tokens = columns[0].shape[-2]
+    width, total = w_qkv.shape
+    count = len(columns)
+    pieces = list(pieces_of(columns))
+    steps = len(pieces) // 2
 
     def kernel(*refs):
-        w_ref, out_ref, acc_ref = refs[3], refs[-2], refs[-1]
-        for step, (array, part) in enumerate(pieces):
+        w_ref, (out_ref, done_ref, acc_ref) = refs[count], refs[-3:]
+        for step in range(steps):
 
             @pl.when(pl.program_id(0) == step)
             def _():
-                product = dot(refs[array][:, part * half : (part + 1) * half], w_ref[...], NT)
+                both = [piece(refs, *where) for where in pieces[2 * step : 2 * step + 2]]
+                product = dot(jnp.concatenate(both, axis=1), w_ref[...], NT)
                 if step == 0:
                     acc_ref[...] = product
-                elif step < len(pieces) - 1:
+                elif step < steps - 1:
                     acc_ref[...] += product
                 else:
                     out_ref[...] = (acc_ref[...] + product).astype(BF)
-
-    whole = pl.BlockSpec((tokens, width), lambda g: (0, 0))
+                    done_ref[...] = jnp.zeros_like(done_ref)
+
     return pl.pallas_call(
         kernel,
-        grid=(len(pieces),),
-        in_specs=[whole, whole, whole, pl.BlockSpec((width, half), lambda g: (0, g))]
+        grid=(steps,),
+        in_specs=[pl.BlockSpec(memory_space=pltpu.VMEM)] * count
+        + [pl.BlockSpec((width, total // steps), lambda g: (0, g))]
         + [pl.BlockSpec(memory_space=pl.ANY)] * len(after),
-        out_specs=whole,
-        out_shape=jax.ShapeDtypeStruct((tokens, width), BF),
+        out_specs=[
+            pl.BlockSpec((tokens, width), lambda g: (0, 0)),
+            pl.BlockSpec((8, LANES), lambda g: (0, 0)),
+        ],
+        out_shape=[
+            jax.ShapeDtypeStruct((tokens, width), BF),
+            jax.ShapeDtypeStruct((8, LANES), F32),
+        ],
         scratch_shapes=[pltpu.VMEM((tokens, width), F32)],
         compiler_params=pltpu.CompilerParams(vmem_limit_bytes=24 * MIB),
         cost_estimate=pl.CostEstimate(flops=4 * 10**9, bytes_accessed=MIB, transcendentals=0),
-    )(dq, dkv_1, dkv_2, w_qkv, *after)
+    )(*columns, w_qkv, *after)
 
 
 def row_blocks(place, own, orders, after):
@@ -477,71 +489,96 @@
     return on_chip(kernel, [out, out], [left, right], after=after, place=[place])
 
 
-def merge_sides(place, left, right, rim_a, rim_b, band_rows, band_cols, after=()):
+def merge_sides(place, lefts, rights, rim_a, rim_b, band_rows, band_cols, after=()):
     edge = MARGIN * band_cols
-
-    def kernel(place_ref, left_ref, right_ref, a_ref, b_ref, ol_ref, or_ref):
+    calls = len(lefts)
+    slots = rim_a.shape[0]
+    each = slots // calls
+
+    def kernel(place_ref, *refs):
+        sides = refs[:calls], refs[calls : 2 * calls]
+        a_ref, b_ref, *outs = refs[2 * calls :]
         even = place_ref[1] == 0
-        for part in range(2):
-            for col in range(2 * MARGIN):
-                source, target = (left_ref, ol_ref) if col < MARGIN else (right_ref, or_ref)
-                base = (col % MARGIN) * band_rows
-                pair = slice(edge + (col // 2) * 2 * EDGE_R, edge + (col // 2 + 1) * 2 * EDGE_R)
-                odd = slice((col % 2) * EDGE_R, (col % 2 + 1) * EDGE_R)
-                rows = source[part, base : base + band_rows, :].astype(F32)
-                rim_a, rim_b = (ref[part, pair, :].astype(F32)[odd] for ref in (a_ref, b_ref))
-                first = rows[:EDGE_R] + jnp.where(even, rim_b, rim_a)
-                last = rows[band_rows - EDGE_R :] + jnp.where(even, rim_a, rim_b)
-                target[part, base : base + band_rows, :] = jnp.concatenate(
-                    [first, rows[EDGE_R : band_rows - EDGE_R], last], axis=0
-                ).astype(BF)
-
-    out = [(left.shape, BF), (right.shape, BF)]
-    return on_chip(kernel, out, [left, right, rim_a, rim_b], after=after, place=[place])
-
-
-def finish(place, mid, rim_a, rim_b, left, right, band_rows, band_cols, after, flops):
-    _, tokens, width = mid.shape
+        for slot in range(slots):
+            for part in range(2):
+                for col in range(2 * MARGIN):
+                    source = sides[col // MARGIN][slot // each]
+                    base = (col % MARGIN) * band_rows
+                    pair = slice(edge + (col // 2) * 2 * EDGE_R, edge + (col // 2 + 1) * 2 * EDGE_R)
+                    odd = slice((col % 2) * EDGE_R, (col % 2 + 1) * EDGE_R)
+                    rows = source[slot % each, part, base : base + band_rows, :].astype(F32)
+                    from_a, from_b = (
+                        ref[slot, part, pair, :].astype(F32)[odd] for ref in (a_ref, b_ref)
+                    )
+                    first = rows[:EDGE_R] + jnp.where(even, from_b, from_a)
+                    last = rows[band_rows - EDGE_R :] + jnp.where(even, from_a, from_b)
+                    outs[col // MARGIN][slot, part, base : base + band_rows, :] = jnp.concatenate(
+                        [first, rows[EDGE_R : band_rows - EDGE_R], last], axis=0
+                    ).astype(BF)
+
+    out = ((slots,) + lefts[0].shape[1:], BF)
+    return on_chip(kernel, [out, out], [*lefts, *rights, rim_a, rim_b], after, place=[place])
+
+
+def finish(place, mids, rim_a, rim_b, left, right, parts, band_rows, band_cols, after, flops):
+    calls = len(mids)
+    slots, _, _, block = rim_a.shape
+    each = slots // calls
     edge = MARGIN * band_cols
-
-    def kernel(place_ref, mid_ref, a_ref, b_ref, left_ref, right_ref, out_ref, acc_ref):
+    tokens = band_rows * band_cols
+
+    def kernel(place_ref, *refs):
+        a_ref, b_ref, left_ref, right_ref, *outs, acc_ref = refs[calls:]
         even = place_ref[1] == 0
-        for part in range(2):
-            for block in range(width // (2 * LANES)):
-                for lane in range(2):
-                    at = slice((2 * block + lane) * LANES, (2 * block + lane + 1) * LANES)
-                    acc_ref[lane] = mid_ref[part, :, at].astype(F32)
-                    from_a, from_b = (r[part, :edge, at].astype(F32) for r in (a_ref, b_ref))
+        for out_ref, part in zip(outs, parts):
+            for slot in range(slots):
+                for lane, at in lanes_of(block):
+                    acc_ref[lane] = refs[slot // each][slot % each, part, :, at].astype(F32)
+                    from_a, from_b = (
+                        r[slot, part, :edge, at].astype(F32) for r in (a_ref, b_ref)
+                    )
                     acc_ref[lane, :edge, :] += jnp.where(even, from_b, from_a)
                     acc_ref[lane, tokens - edge :, :] += jnp.where(even, from_a, from_b)
                     for col in range(MARGIN):
                         here = slice(col * band_rows, (col + 1) * band_rows)
                         first = pl.ds(col, band_rows, stride=band_cols)
                         last = pl.ds(band_cols - MARGIN + col, band_rows, stride=band_cols)
-                        acc_ref[lane, first, :] += left_ref[part, here, at].astype(F32)
-                        acc_ref[lane, last, :] += right_ref[part, here, at].astype(F32)
-                both = jnp.concatenate([acc_ref[0], acc_ref[1]], axis=1).astype(BF)
-                start = part * width + block * 2 * LANES
-                out_ref[:, start : start + 2 * LANES] = both
-
-    out = [((tokens, 2 * width), BF)]
-    scratch = [pltpu.VMEM((2, tokens, LANES), F32)]
-    operands = [mid, rim_a, rim_b, left, right]
-    return on_chip(kernel, out, operands, after, scratch, flops, [place])[0]
+                        acc_ref[lane, first, :] += left_ref[slot, part, here, at].astype(F32)
+                        acc_ref[lane, last, :] += right_ref[slot, part, here, at].astype(F32)
+                    start = slot * block + lane * LANES
+                    out_ref[:, start : start + LANES] = acc_ref[lane].astype(BF)
+
+    out = [((tokens, slots * block), BF)] * len(parts)
+    scratch = [pltpu.VMEM((block // LANES, tokens, LANES), F32)]
+    operands = [*mids, rim_a, rim_b, left, right]
+    return on_chip(kernel, out, operands, after, scratch, flops, [place])
+
+
+def pieces_of(arrays):
+    for i, array in enumerate(arrays):
+        slots = range(array.shape[0]) if array.ndim == 3 else [None]
+        for slot in slots:
+            for start in range(0, array.shape[-1], 2 * LANES):
+                yield i, slot, start
+
+
+def piece(refs, i, slot, start):
+    here = slice(start, start + 2 * LANES)
+    return refs[i][:, here] if slot is None else refs[i][slot, :, here]
 
 
 def grad_rows(rows, columns, scale, kind, after=()):
     features, count = rows.shape[0], len(columns)
-    width = columns[0].shape[1]
+    pieces = list(pieces_of(columns))
 
     def kernel(rows_ref, *refs):
-        for i, columns_ref in enumerate(refs[:count]):
-            for start in range(0, width, 2 * LANES):
-                part = dot(rows_ref[...], columns_ref[:, start : start + 2 * LANES])
-                at = i * width + start
-                refs[count][:, at : at + 2 * LANES] = (part * scale).astype(kind)
-
-    return on_chip(kernel, [((features, count * width), kind)], [rows, *columns], after)[0]
+        for at, where in enumerate(pieces):
+            part = dot(rows_ref[...], piece(refs, *where))
+            here = slice(at * 2 * LANES, (at + 1) * 2 * LANES)
+            refs[count][:, here] = (part * scale).astype(kind)
+
+    out = [((features, len(pieces) * 2 * LANES), kind)]
+    return on_chip(kernel, out, [rows, *columns], after)[0]
 
 
 def add_split(keep, received, after=()):
@@ -552,20 +589,6 @@
         send_ref[...] = (keep_ref[half:, :] + received_ref[half:, :].astype(F32)).astype(BF)
 
     return on_chip(kernel, [((half, columns), F32), ((half, columns), BF)], [keep, received], after)
-
-
-def add_blocks(place, keep, received, blocks, after):
-    rows, columns = keep.shape
-    size = rows // blocks
-
-    def kernel(place_ref, keep_ref, received_ref, send_ref):
-        me = place_ref[2] & (blocks - 1)
-        for b in range(blocks):
-            here = slice(b * size, (b + 1) * size)
-            send_ref[me ^ b] = (keep_ref[here, :] + received_ref[here, :].astype(F32)).astype(BF)
-
-    out = [((blocks, size, columns), BF)]
-    return on_chip(kernel, out, [keep, received], after, place=[place])[0]
 
 
 def sent_blocks(keep, received, blocks, after):
@@ -583,7 +606,7 @@
     return on_chip(kernel, out, [keep, received], after)
 
 
-def gather_sums(groups, places, width, flops):
+def gather_sums(groups, places, width, after, flops):
     flat = [array for group in groups for array in group]
 
     def kernel(*refs):
@@ -597,7 +620,7 @@
                 parts = [ref[i, :, here].astype(F32) for ref in mine for i in range(ref.shape[0])]
                 out_ref[:, target : target + size] = functools.reduce(lambda a, b: a + b, parts)
 
-    return on_chip(kernel, [((flat[0].shape[1], width), F32)], flat, flops=flops)[0]
+    return on_chip(kernel, [((flat[0].shape[1], width), F32)], flat, after, flops=flops)[0]
 
 
 def shifted(array, axis, by, wrap):
@@ -681,56 +704,59 @@
     scale = float(tokens * n_dp * n_lat * n_lon) ** -0.5
 
     attend = lambda first, count, before, after: attention_grads(
-        first, count, slots, start, masks, halo, qkv, flat_grad, w_qkv, shape, before, after
+        first, count, start, masks, halo, qkv, flat_grad, w_qkv, shape, before, after
     )
 
-    def return_sides(grads, rims, after):
+    def return_sides(calls, rims, after):
         to_left, to_right = merge_sides(
-            start, grads[4], grads[5], *rims, band_rows, band_cols, after
+            start, [c[4] for c in calls], [c[5] for c in calls], *rims, band_rows, band_cols, after
         )
         from_right = shifted(to_left, "lon", -1, True)
         from_left = shifted(to_right, "lon", 1, True)
         return to_left, from_left, from_right
 
+    def finished(calls, rims, sides, parts, after, flops):
+        mids = [c[3] for c in calls]
+        return finish(start, mids, *rims, *sides, parts, band_rows, band_cols, after, flops)
+
+    groups = HEADS // GROUP
     one = attend(0, slots, [], [])
     rims_1 = swapped(one[1], one[2], "lat")
-    two = attend(slots, 1, [(0, one[0])], [])
-    sent, *sides_1 = return_sides(one, rims_1, [two[1]])
-    two = attend(slots + 1, 1, list(enumerate(two)), [sent])
-    rims_2 = swapped(two[1], two[2], "lat")
-    dq = two[0]
-
-    dkv_1 = finish(start, one[3], *rims_1, *sides_1, band_rows, band_cols, [dq], 2 * 10**9)
-    sent, *sides_2 = return_sides(two, rims_2, [dkv_1])
-    send = grad_rows(rows_send, [dq, dkv_1], scale, BF, after=[sent])
+    two = attend(slots, groups - slots - 1, [], [one[0]])
+    sent, *sides_1 = return_sides([one], rims_1, [two[0]])
+    three = attend(groups - 1, 1, [two[1], two[2]], [sent])
+    rims_2 = swapped(three[1], three[2], "lat")
+    dq = [one[0], two[0], three[0]]
+
+    dk_1, dv_1 = finished([one], rims_1, sides_1, (0, 1), [three[0]], 2 * 10**9)
+    sent, *sides_2 = return_sides([two, three], rims_2, [dk_1])
+    send = grad_rows(rows_send, [*dq, dk_1, dv_1], scale, BF, after=[sent])
     received = exchanged(send, *first)
-    keep = grad_rows(rows_keep, [dq, dkv_1], scale, F32, after=[send])
+    keep = grad_rows(rows_keep, [*dq, dk_1, dv_1], scale, F32, after=[send])
     keep, send = add_split(keep, received)
 
-    dkv_2 = finish(start, two[3], *rims_2, *sides_2, band_rows, band_cols, [keep], FINISH_FLOPS)
+    (dk_2,) = finished([two, three], rims_2, sides_2, (0,), [keep], FINISH_FLOPS)
     for stage in stages[:-1]:
-        keep, send = add_split(keep, exchanged_stage(send, stage), [dkv_2])
-    send_2 = grad_rows(rows_send, [dkv_2], scale, BF, after=[keep])
+        keep, send = add_split(keep, exchanged_stage(send, stage), [dk_2])
     received = exchanged_stage(send, stages[-1])
+    (dv_2,) = finished([two, three], rims_2, sides_2, (1,), [keep], 10**5)
+    send_2 = grad_rows(rows_send, [dk_2, dv_2], scale, BF)
     received_2 = exchanged(send_2, *first)
-    keep_2 = grad_rows(rows_keep, [dkv_2], scale, F32, after=[send_2])
-    keep_2, send_2 = add_split(keep_2, received_2)
-    received_2 = exchanged_stage(send_2, stages[0])
-    grad_inputs = input_grads(dq, dkv_1, dkv_2, w_qkv, [send_2])
-    keep, *send = sent_blocks(keep, received, n_lon, [grad_inputs])
+    keep_2 = grad_rows(rows_keep, [dk_2, dv_2], scale, F32, after=[send_2])
+    keep, *send = sent_blocks(keep, received, n_lon, [keep_2])
     group_1 = [keep] + [exchanged(a, "lon", i + 1) for i, a in enumerate(send)]
-    group_1 = [gather_sums([group_1], [[(0, 2 * width, 0)]], 2 * width, GATHER_FLOPS)[None]]
-    for stage in stages[1:]:
+    sum_1 = gather_sums([group_1], [[(0, 2 * width, 0)]], 2 * width, [], GATHER_FLOPS)[None]
+    for stage in stages:
         keep_2, send_2 = add_split(keep_2, received_2, [keep])
         received_2 = exchanged_stage(send_2, stage)
-    send_2 = add_blocks(start, keep_2, received_2, n_lon, group_1)
-    group_2 = [lax.all_to_all(send_2, "lon", 0, 0, tiled=True)]
+    keep_2, *send_2 = sent_blocks(keep_2, received_2, n_lon, [sum_1])
+    group_2 = [keep_2] + [exchanged(a, "lon", i + 1) for i, a in enumerate(send_2)]
+    grad_inputs, done = input_grads([*dq, dk_1, dk_2, dv_1, dv_2], w_qkv, [keep_2])
     places = [
         [(0, width, 0), (width, half, width), (width + half, half, 2 * width)],
         [(0, half, width + half), (half, half, 2 * width + half)],
     ]
-    grad_w = gather_sums([group_1, group_2], places, 3 * width, 10**5)
-
+    grad_w = gather_sums([[sum_1], group_2], places, 3 * width, [done], 10**5)
     return (grad_inputs.reshape(inputs.shape), grad_w)
 
 

time: 159 us -> 155 us (0.975)
  blocking collectives: 11.9 us -> 0 us
  waiting for transfers between devices: 25.1 us -> 31.2 us
  starting transfers between devices: 41.4 us -> 45.7 us
    all_to_all x1 -> x0, blocking collectives: 11.9 us -> none  [body(): group_2 = [lax.all_to_all(send_2, 'lon', 0, 0, tiled=True)]]
    ppermute x4, waiting for transfers between devices: 2.38 us -> 10.8 us  [exchanged_stage(): return lax.ppermute(array, ('dp', 'lat'), route)]
    ppermute x5 -> x8, starting transfers between devices: 8.65 us -> 12.9 us  [exchanged(): lax.ppermute(array, axis, [(i, i ^ flip) for i in range(lax.axis_size(axi...]
    ppermute x5 -> x8, waiting for transfers between devices: 6.33 us -> 3.94 us  [exchanged(): lax.ppermute(array, axis, [(i, i ^ flip) for i in range(lax.axis_size(axi...]
    unnamed x24 -> x22, local copies, waits for them, and re-layouts: 6.49 us -> 5.27 us
    pallas_call x20 -> x21, Pallas kernels: 15.9 us -> 15.9 us  [on_chip(): pl.pallas_call(run, in_specs=[pl.BlockSpec(memory_space=pltpu.SMEM)] * le...]
  transfers between devices with their start and end apart: 23 -> 26, of which waited for: 8 -> 9; matrix products, arithmetic and copies ran while one was open for 0% -> 0% of each run, Pallas kernels for 29% -> 29%
where the time goes in v1:
time: 155 us
  Pallas kernels  71.8 us (46%)
  starting transfers between devices  45.7 us (29%)
  waiting for transfers between devices  31.2 us (20%)
  local copies, waits for them, and re-layouts  5.27 us (3%)
    pallas_call x3, Pallas kernels, attention_grads(): pl.pallas_call(functools.partial(attention_kernel, band_rows, band_cols,...  40.9 us
    ppermute x6, waiting for transfers between devices, shifted(): return lax.ppermute(array, axis, route)  16.1 us
    pallas_call x21, Pallas kernels, on_chip(): pl.pallas_call(run, in_specs=[pl.BlockSpec(memory_space=pltpu.SMEM)] * le...  15.9 us
    ppermute x8, starting transfers between devices, swapped(): lax.ppermute(array, axis, route(pairs[offset::2]))  13.3 us
    ppermute x8, starting transfers between devices, exchanged(): lax.ppermute(array, axis, [(i, i ^ flip) for i in range(lax.axis_size(axi...  12.9 us
    ppermute x6, starting transfers between devices, shifted(): return lax.ppermute(array, axis, route)  12.8 us
    ppermute x4, waiting for transfers between devices, exchanged_stage(): return lax.ppermute(array, ('dp', 'lat'), route)  10.8 us
    ppermute x4, starting transfers between devices, exchanged_stage(): return lax.ppermute(array, ('dp', 'lat'), route)  6.62 us
  transfers between devices with their start and end apart: 26, of which 9 were waited for; matrix products, arithmetic and copies ran while one was open for 0% of the time, Pallas kernels for 29%

profile of v1, /device:TPU:0, one launch (start us, length us, event | category | flops | bytes accessed | tf_op | source)
XLA Modules:
  0.0 155.0 jit_solution(3191494325771408166)
XLA Ops:
  3.4 5.0 %collective-permute-start.1 = (bf16[192,1024]{1,0:T(8,128)(2,1)}, bf16[192,1024]{1,0:T(8,128)(2,1)S(1)}, u32[]{:S(2)}, u32[]{:S(2)}) collective-permute-start(bf16[192,1024]{1,0:T(8,128)(2,1)} %get-tuple-element.53), channel_id=1, source_target_pairs={{0,3},{1,0},{2,1},{3,2},{4,7},{5,4},{6,5},{7,6},{8,11},{9,8},{10,9... | collective-permute-start | bytes 1179656 | tf_op jit(solution)/shard_map/ppermute | solution.py:629
  13.4 4.0 %shard_map.50.refs_3_.refs_1_ = bf16[8,512,128]{2,1,0:T(8,128)(2,1)} custom-call(s32[3]{0:T(128)} %copy-done.6), custom_call_target="tpu_custom_call" | custom-call | flops 10000000 | bytes 2097152 | tf_op jit(solution)/shard_map/pallas_call | solution.py:70
  17.4 2.8 %copy-done.4 = bf16[1024,3072]{1,0:T(8,128)(2,1)S(1)} copy-done((bf16[1024,3072]{1,0:T(8,128)(2,1)S(1)}, bf16[1024,3072]{1,0:T(8,128)(2,1)}, u32[]{:S(2)}) %copy-start.4) | copy-done | bytes 6291480
  20.2 4.9 %shard_map.53.refs_4_.refs_8_ = bf16[512,3072]{1,0:T(8,128)(2,1)S(1)} custom-call(bf16[512,1024]{1,0:T(8,128)(2,1)S(1)} %bitcast.10, bf16[1024,3072]{1,0:T(8,128)(2,1)S(1)} %copy-done.4, bf16[192,1024]{1,0:T(8,128)(2,1)S(1)} %get-tuple-element.52.refs_2_.refs_0_), custom_call_target="tpu_custom_call" | custom-call | flops 1000000000 | bytes 1048576 | tf_op jit(solution)/shard_map/pallas_call | solution.py:352
  27.0 2.0 %collective-permute-start.4 = (bf16[96,1024]{1,0:T(8,128)(2,1)S(1)}, bf16[96,1024]{1,0:T(8,128)(2,1)S(1)}, u32[]{:S(2)}, u32[]{:S(2)}) collective-permute-start(bf16[96,1024]{1,0:T(8,128)(2,1)S(1)} %get-tuple-element.58), channel_id=1, source_target_pairs={{0,4},{8,12},{4,0},{12,8},{1,5},{9,13},{5,1},{13,9},{2,6},{10,14},... | collective-permute-start | bytes 589832 | tf_op jit(solution)/shard_map/ppermute | solution.py:637
  30.0 19.4 %shard_map.56 = (bf16[2,512,256]{2,1,0:T(8,128)(2,1)S(1)}, bf16[2,2,192,256]{3,2,1,0:T(8,128)(2,1)S(1)}, bf16[2,2,192,256]{3,2,1,0:T(8,128)(2,1)S(1)}, bf16[2,2,...) custom-call(s32[3]{0:T(128)S(1)} %copy-done.7, ...), custom_call_target="tpu_custom_call" | custom-call | flops 28000000000 | bytes 16777216 | tf_op jit(solution)/shard_map/pallas_call | solution.py:286
  49.5 6.0 %collective-permute-start.6 = (bf16[2,2,192,256]{3,2,1,0:T(8,128)(2,1)S(1)}, bf16[2,2,192,256]{3,2,1,0:T(8,128)(2,1)S(1)}, u32[]{:S(2)}, u32[]{:S(2)}) collective-permute-start(bf16[2,2,192,256]{3,2,1,0:T(8,128)(2,1)S(1)} %get-tuple-element.66), channel_id=1, source_target_pairs={{0,4},{8,12},{4,0},{12,8},{1,5},{9,13},{5,1},{13,9},{2,6},{10,14},... | collective-permute-start | bytes 1179656 | tf_op jit(solution)/shard_map/ppermute | solution.py:637
  56.3 10.7 %shard_map.57 = (bf16[1,512,256]{2,1,0:T(8,128)(2,1)S(1)}, bf16[1,2,192,256]{3,2,1,0:T(8,128)(2,1)S(1)}, bf16[1,2,192,256]{3,2,1,0:T(8,128)(2,1)S(1)}, bf16[1,2,...) custom-call(s32[3]{0:T(128)S(1)} %copy-done.7, ...), custom_call_target="tpu_custom_call" | custom-call | flops 14000000000 | bytes 8388608 | tf_op jit(solution)/shard_map/pallas_call | solution.py:286
  68.0 3.7 %collective-permute-start.9 = (bf16[2,2,192,256]{3,2,1,0:T(8,128)(2,1)S(1)}, bf16[2,2,192,256]{3,2,1,0:T(8,128)(2,1)S(1)}, u32[]{:S(2)}, u32[]{:S(2)}) collective-permute-start(bf16[2,2,192,256]{3,2,1,0:T(8,128)(2,1)S(1)} %get-tuple-element.68.refs_13_), channel_id=1, source_target_pairs={{0,3},{1,0},{2,1},{3,2},{4,7},{5,4},{6,5},{7,6},{8,11},{9,8},{10,9... | collective-permute-start | bytes 1179656 | tf_op jit(solution)/shard_map/ppermute | solution.py:629
  71.7 10.7 %shard_map.59 = (bf16[1,512,256]{2,1,0:T(8,128)(2,1)S(1)}, bf16[2,2,192,256]{3,2,1,0:T(8,128)(2,1)S(1)}, bf16[2,2,192,256]{3,2,1,0:T(8,128)(2,1)S(1)}, bf16[1,2,...) custom-call(s32[3]{0:T(128)S(1)} %copy-done.7, ...), custom_call_target="tpu_custom_call" | custom-call | flops 14000000000 | bytes 8388608 | tf_op jit(solution)/shard_map/pallas_call | solution.py:286
  85.0 2.3 %collective-permute-done.9.refs_5_ = bf16[2,2,192,256]{3,2,1,0:T(8,128)(2,1)S(1)} collective-permute-done((bf16[2,2,192,256]{3,2,1,0:T(8,128)(2,1)S(1)}, bf16[2,2,192,256]{3,2,1,0:T(8,128)(2,1)S(1)}, u32[]{:S(2)}, u32[]{:S(2)}) %collective-permute-start.9) | collective-permute-done | bytes 393248 | tf_op jit(solution)/shard_map/ppermute | solution.py:629
  87.3 1.9 %shard_map.60 = (bf16[512,512]{1,0:T(8,128)(2,1)S(1)}, bf16[512,512]{1,0:T(8,128)(2,1)S(1)}) custom-call(s32[3]{0:T(128)S(1)} %copy-done.7, bf16[2,2,512,256]{3,2,1,0:T(8,128)(2,1)S(1)} %get-tuple-element.70.refs_1_, bf16[2,2,192,256]{3,2,1,0:T(8,128)(2,1)S(1)} %collective-permute-done.6.refs_3_.refs_2_, ...), custom_call_target="tpu_custom_call" | custom-call | flops 2000000000 | bytes 10000 | tf_op jit(solution)/shard_map/pallas_call | solution.py:327
  91.2 4.0 %collective-permute-start.14 = (bf16[512,2048]{1,0:T(8,128)(2,1)S(1)}, bf16[512,2048]{1,0:T(8,128)(2,1)S(1)}, u32[]{:S(2)}, u32[]{:S(2)}) collective-permute-start(bf16[512,2048]{1,0:T(8,128)(2,1)S(1)} %shard_map.62.refs_6_), channel_id=1, source_target_pairs={{0,4},{4,0},{8,12},{12,8},{1,5},{5,1},{9,13},{13,9},{2,6},{6,2},{1... | collective-permute-start | bytes 6291464 | tf_op jit(solution)/shard_map/ppermute | solution.py:643
  95.2 3.8 %collective-permute-start.13 = (bf16[2,2,192,256]{3,2,1,0:T(8,128)(2,1)S(1)}, bf16[2,2,192,256]{3,2,1,0:T(8,128)(2,1)S(1)}, u32[]{:S(2)}, u32[]{:S(2)}) collective-permute-start(bf16[2,2,192,256]{3,2,1,0:T(8,128)(2,1)S(1)} %get-tuple-element.82.refs_6_), channel_id=1, source_target_pairs={{0,3},{1,0},{2,1},{3,2},{4,7},{5,4},{6,5},{7,6},{8,11},{9,8},{10,9... | collective-permute-start | bytes 1179656 | tf_op jit(solution)/shard_map/ppermute | solution.py:629
  102.2 6.8 %collective-permute-done.12.refs_5_ = bf16[2,2,192,256]{3,2,1,0:T(8,128)(2,1)S(1)} collective-permute-done((bf16[2,2,192,256]{3,2,1,0:T(8,128)(2,1)S(1)}, bf16[2,2,192,256]{3,2,1,0:T(8,128)(2,1)S(1)}, u32[]{:S(2)}, u32[]{:S(2)}) %collective-permute-start.12) | collective-permute-done | bytes 393248 | tf_op jit(solution)/shard_map/ppermute | solution.py:629
  109.0 5.8 %collective-permute-done.13.refs_6_ = bf16[2,2,192,256]{3,2,1,0:T(8,128)(2,1)S(1)} collective-permute-done((bf16[2,2,192,256]{3,2,1,0:T(8,128)(2,1)S(1)}, bf16[2,2,192,256]{3,2,1,0:T(8,128)(2,1)S(1)}, u32[]{:S(2)}, u32[]{:S(2)}) %collective-permute-start.13) | collective-permute-done | bytes 393248 | tf_op jit(solution)/shard_map/ppermute | solution.py:629
  118.3 1.7 %collective-permute-start.17 = (bf16[128,2048]{1,0:T(8,128)(2,1)S(1)}, bf16[128,2048]{1,0:T(8,128)(2,1)S(1)}, u32[]{:S(2)}, u32[]{:S(2)}) collective-permute-start(bf16[128,2048]{1,0:T(8,128)(2,1)S(1)} %get-tuple-element.87), channel_id=1, source_target_pairs={{0,8},{4,20},{8,0},{12,28},{16,24},{20,4},{24,16},{28,12},{1,9},{5... | collective-permute-start | bytes 1572872 | tf_op jit(solution)/shard_map/ppermute | solution.py:676
  120.7 6.8 %collective-permute-done.17.refs_1_ = bf16[128,2048]{1,0:T(8,128)(2,1)S(1)} collective-permute-done((bf16[128,2048]{1,0:T(8,128)(2,1)S(1)}, bf16[128,2048]{1,0:T(8,128)(2,1)S(1)}, u32[]{:S(2)}, u32[]{:S(2)}) %collective-permute-start.17) | collective-permute-done | bytes 524320 | tf_op jit(solution)/shard_map/ppermute | solution.py:676
  130.1 1.9 %collective-permute-start.21 = (bf16[1,32,2048]{2,1,0:T(8,128)(2,1)S(1)}, bf16[1,32,2048]{2,1,0:T(8,128)(2,1)S(1)}, u32[]{:S(2)}, u32[]{:S(2)}) collective-permute-start(bf16[1,32,2048]{2,1,0:T(8,128)(2,1)S(1)} %get-tuple-element.94), channel_id=1, source_target_pairs={{0,2},{1,3},{2,0},{3,1},{4,6},{5,7},{6,4},{7,5},{8,10},{9,11},{10,... | collective-permute-start | bytes 393224 | tf_op jit(solution)/shard_map/ppermute | solution.py:643
  132.0 1.8 %collective-permute-start.22 = (bf16[1,32,2048]{2,1,0:T(8,128)(2,1)S(1)}, bf16[1,32,2048]{2,1,0:T(8,128)(2,1)S(1)}, u32[]{:S(2)}, u32[]{:S(2)}) collective-permute-start(bf16[1,32,2048]{2,1,0:T(8,128)(2,1)S(1)} %get-tuple-element.95), channel_id=1, source_target_pairs={{0,3},{1,2},{2,1},{3,0},{4,7},{5,6},{6,5},{7,4},{8,11},{9,10},{10,... | collective-permute-start | bytes 393224 | tf_op jit(solution)/shard_map/ppermute | solution.py:643
  133.8 3.3 %collective-permute-done.18.refs_1_ = bf16[256,1024]{1,0:T(8,128)(2,1)S(1)} collective-permute-done((bf16[256,1024]{1,0:T(8,128)(2,1)S(1)}, bf16[256,1024]{1,0:T(8,128)(2,1)S(1)}, u32[]{:S(2)}, u32[]{:S(2)}) %collective-permute-start.18) | collective-permute-done | bytes 524320 | tf_op jit(solution)/shard_map/ppermute | solution.py:676
  137.2 1.7 %collective-permute-start.19 = (bf16[128,1024]{1,0:T(8,128)(2,1)S(1)}, bf16[128,1024]{1,0:T(8,128)(2,1)S(1)}, u32[]{:S(2)}, u32[]{:S(2)}) collective-permute-start(bf16[128,1024]{1,0:T(8,128)(2,1)S(1)} %get-tuple-element.92), channel_id=1, source_target_pairs={{0,8},{4,20},{8,0},{12,28},{16,24},{20,4},{24,16},{28,12},{1,9},{5... | collective-permute-start | bytes 786440 | tf_op jit(solution)/shard_map/ppermute | solution.py:676
  138.9 3.9 %collective-permute-done.21.refs_2_ = bf16[1,32,2048]{2,1,0:T(8,128)(2,1)S(1)} collective-permute-done((bf16[1,32,2048]{2,1,0:T(8,128)(2,1)S(1)}, bf16[1,32,2048]{2,1,0:T(8,128)(2,1)S(1)}, u32[]{:S(2)}, u32[]{:S(2)}) %collective-permute-start.21) | collective-permute-done | bytes 131104 | tf_op jit(solution)/shard_map/ppermute | solution.py:643
  148.1 6.1 %shard_map.75 = (bf16[512,1024]{1,0:T(8,128)(2,1)}, f32[8,128]{1,0:T(8,128)S(1)}) custom-call(bf16[2,512,256]{2,1,0:T(8,128)(2,1)S(1)} %get-tuple-element.60.refs_11_.refs_1_.refs_0_, bf16[1,512,256]{2,1,0:T(8,128)(2,1)S(1)} %get-tuple-element.61.refs_5_.refs_2_.refs_1_, bf16[1,512,256]{2,1,0:T(8,128)(2,1)S(1)} %get-tuple-element.69.refs_6_.refs_3_.refs_2_, ...), custom_call_target="tpu_custom_call" | custom-call | flops 4000000000 | bytes 1048576 | tf_op jit(solution)/shard_map/pallas_call | solution.py:390
  (79 shorter events, 33.0 us)
Async XLA Ops:
  3.4 21.7 %collective-permute-start.1 = (bf16[192,1024]{1,0:T(8,128)(2,1)}, bf16[192,1024]{1,0:T(8,128)(2,1)S(1)}, u32[]{:S(2)}, u32[]{:S(2)}) collective-permute-start(bf16[192,1024]{1,0:T(8,128)(2,1)} %get-tuple-element.53), channel_id=1, source_target_pairs={{0,3},{1,0},{2,1},{3,2},{4,7},{5,4},{6,5},{7,6},{8,11},{9,8},{10,9... | collective-permute-start | bytes 1179656 | tf_op jit(solution)/shard_map/ppermute | solution.py:629
  8.4 17.9 %collective-permute-start = (bf16[192,1024]{1,0:T(8,128)(2,1)S(1)}, bf16[192,1024]{1,0:T(8,128)(2,1)S(1)}, u32[]{:S(2)}, u32[]{:S(2)}) collective-permute-start(bf16[192,1024]{1,0:T(8,128)(2,1)S(1)} %get-tuple-element.52.refs_2_.refs_0_), channel_id=1, source_target_pairs={{0,1},{1,2},{2,3},{3,0},{4,5},{5,6},{6,7},{7,4},{8,9},{9,10},{10,1... | collective-permute-start | bytes 1179656 | tf_op jit(solution)/shard_map/ppermute | solution.py:629
  11.0 18.6 %collective-permute-start.2 = (bf16[96,1024]{1,0:T(8,128)(2,1)}, bf16[96,1024]{1,0:T(8,128)(2,1)S(1)}, u32[]{:S(2)}, u32[]{:S(2)}) collective-permute-start(bf16[96,1024]{1,0:T(8,128)(2,1)} %get-tuple-element.54), channel_id=1, source_target_pairs={{0,4},{8,12},{4,0},{12,8},{1,5},{9,13},{5,1},{13,9},{2,6},{10,14},... | collective-permute-start | bytes 589832 | tf_op jit(solution)/shard_map/ppermute | solution.py:637
  11.0 18.6 %collective-permute-start.3 = (bf16[96,1024]{1,0:T(8,128)(2,1)}, bf16[96,1024]{1,0:T(8,128)(2,1)}, u32[]{:S(2)}, u32[]{:S(2)}) collective-permute-start(bf16[96,1024]{1,0:T(8,128)(2,1)} %get-tuple-element.55), channel_id=1, source_target_pairs={{4,8},{8,4},{5,9},{9,5},{6,10},{10,6},{7,11},{11,7},{20,24},{24,20... | collective-permute-start | bytes 589832 | tf_op jit(solution)/shard_map/ppermute | solution.py:637
  49.5 17.6 %collective-permute-start.6 = (bf16[2,2,192,256]{3,2,1,0:T(8,128)(2,1)S(1)}, bf16[2,2,192,256]{3,2,1,0:T(8,128)(2,1)S(1)}, u32[]{:S(2)}, u32[]{:S(2)}) collective-permute-start(bf16[2,2,192,256]{3,2,1,0:T(8,128)(2,1)S(1)} %get-tuple-element.66), channel_id=1, source_target_pairs={{0,4},{8,12},{4,0},{12,8},{1,5},{9,13},{5,1},{13,9},{2,6},{10,14},... | collective-permute-start | bytes 1179656 | tf_op jit(solution)/shard_map/ppermute | solution.py:637
  55.4 11.6 %collective-permute-start.7 = (bf16[2,2,192,256]{3,2,1,0:T(8,128)(2,1)S(1)}, bf16[2,2,192,256]{3,2,1,0:T(8,128)(2,1)S(1)}, u32[]{:S(2)}, u32[]{:S(2)}) collective-permute-start(bf16[2,2,192,256]{3,2,1,0:T(8,128)(2,1)S(1)} %get-tuple-element.67), channel_id=1, source_target_pairs={{4,8},{8,4},{5,9},{9,5},{6,10},{10,6},{7,11},{11,7},{20,24},{24,20... | collective-permute-start | bytes 1179656 | tf_op jit(solution)/shard_map/ppermute | solution.py:637
  67.7 17.2 %collective-permute-start.8 = (bf16[2,2,192,256]{3,2,1,0:T(8,128)(2,1)S(1)}, bf16[2,2,192,256]{3,2,1,0:T(8,128)(2,1)S(1)}, u32[]{:S(2)}, u32[]{:S(2)}) collective-permute-start(bf16[2,2,192,256]{3,2,1,0:T(8,128)(2,1)S(1)} %get-tuple-element.71), channel_id=1, source_target_pairs={{0,1},{1,2},{2,3},{3,0},{4,5},{5,6},{6,7},{7,4},{8,9},{9,10},{10,1... | collective-permute-start | bytes 1179656 | tf_op jit(solution)/shard_map/ppermute | solution.py:629
  68.0 19.2 %collective-permute-start.9 = (bf16[2,2,192,256]{3,2,1,0:T(8,128)(2,1)S(1)}, bf16[2,2,192,256]{3,2,1,0:T(8,128)(2,1)S(1)}, u32[]{:S(2)}, u32[]{:S(2)}) collective-permute-start(bf16[2,2,192,256]{3,2,1,0:T(8,128)(2,1)S(1)} %get-tuple-element.68.refs_13_), channel_id=1, source_target_pairs={{0,3},{1,0},{2,1},{3,2},{4,7},{5,4},{6,5},{7,6},{8,11},{9,8},{10,9... | collective-permute-start | bytes 1179656 | tf_op jit(solution)/shard_map/ppermute | solution.py:629
  82.4 6.8 %collective-permute-start.10 = (bf16[2,2,192,256]{3,2,1,0:T(8,128)(2,1)S(1)}, bf16[2,2,192,256]{3,2,1,0:T(8,128)(2,1)S(1)}, u32[]{:S(2)}, u32[]{:S(2)}) collective-permute-start(bf16[2,2,192,256]{3,2,1,0:T(8,128)(2,1)S(1)} %get-tuple-element.75), channel_id=1, source_target_pairs={{0,4},{8,12},{4,0},{12,8},{1,5},{9,13},{5,1},{13,9},{2,6},{10,14},... | collective-permute-start | bytes 1179656 | tf_op jit(solution)/shard_map/ppermute | solution.py:637
  84.1 5.1 %collective-permute-start.11 = (bf16[2,2,192,256]{3,2,1,0:T(8,128)(2,1)S(1)}, bf16[2,2,192,256]{3,2,1,0:T(8,128)(2,1)S(1)}, u32[]{:S(2)}, u32[]{:S(2)}) collective-permute-start(bf16[2,2,192,256]{3,2,1,0:T(8,128)(2,1)S(1)} %get-tuple-element.76), channel_id=1, source_target_pairs={{4,8},{8,4},{5,9},{9,5},{6,10},{10,6},{7,11},{11,7},{20,24},{24,20... | collective-permute-start | bytes 1179656 | tf_op jit(solution)/shard_map/ppermute | solution.py:637
  91.2 9.1 %collective-permute-start.14 = (bf16[512,2048]{1,0:T(8,128)(2,1)S(1)}, bf16[512,2048]{1,0:T(8,128)(2,1)S(1)}, u32[]{:S(2)}, u32[]{:S(2)}) collective-permute-start(bf16[512,2048]{1,0:T(8,128)(2,1)S(1)} %shard_map.62.refs_6_), channel_id=1, source_target_pairs={{0,4},{4,0},{8,12},{12,8},{1,5},{5,1},{9,13},{13,9},{2,6},{6,2},{1... | collective-permute-start | bytes 6291464 | tf_op jit(solution)/shard_map/ppermute | solution.py:643
  95.2 13.8 %collective-permute-start.12 = (bf16[2,2,192,256]{3,2,1,0:T(8,128)(2,1)S(1)}, bf16[2,2,192,256]{3,2,1,0:T(8,128)(2,1)S(1)}, u32[]{:S(2)}, u32[]{:S(2)}) collective-permute-start(bf16[2,2,192,256]{3,2,1,0:T(8,128)(2,1)S(1)} %get-tuple-element.81), channel_id=1, source_target_pairs={{0,1},{1,2},{2,3},{3,0},{4,5},{5,6},{6,7},{7,4},{8,9},{9,10},{10,1... | collective-permute-start | bytes 1179656 | tf_op jit(solution)/shard_map/ppermute | solution.py:629
  95.2 19.6 %collective-permute-start.13 = (bf16[2,2,192,256]{3,2,1,0:T(8,128)(2,1)S(1)}, bf16[2,2,192,256]{3,2,1,0:T(8,128)(2,1)S(1)}, u32[]{:S(2)}, u32[]{:S(2)}) collective-permute-start(bf16[2,2,192,256]{3,2,1,0:T(8,128)(2,1)S(1)} %get-tuple-element.82.refs_6_), channel_id=1, source_target_pairs={{0,3},{1,0},{2,1},{3,2},{4,7},{5,4},{6,5},{7,6},{8,11},{9,8},{10,9... | collective-permute-start | bytes 1179656 | tf_op jit(solution)/shard_map/ppermute | solution.py:629
  100.6 15.4 %collective-permute-start.15 = (bf16[256,2048]{1,0:T(8,128)(2,1)S(1)}, bf16[256,2048]{1,0:T(8,128)(2,1)S(1)}, u32[]{:S(2)}, u32[]{:S(2)}) collective-permute-start(bf16[256,2048]{1,0:T(8,128)(2,1)S(1)} %get-tuple-element.85), channel_id=1, source_target_pairs={{0,16},{4,12},{8,24},{12,4},{16,0},{20,28},{24,8},{28,20},{1,17},{... | collective-permute-start | bytes 3145736 | tf_op jit(solution)/shard_map/ppermute | solution.py:676
  118.2 9.4 %collective-permute-start.16 = (bf16[512,1024]{1,0:T(8,128)(2,1)S(1)}, bf16[512,1024]{1,0:T(8,128)(2,1)S(1)}, u32[]{:S(2)}, u32[]{:S(2)}) collective-permute-start(bf16[512,1024]{1,0:T(8,128)(2,1)S(1)} %shard_map.68.refs_3_), channel_id=1, source_target_pairs={{0,4},{4,0},{8,12},{12,8},{1,5},{5,1},{9,13},{13,9},{2,6},{6,2},{1... | collective-permute-start | bytes 3145736 | tf_op jit(solution)/shard_map/ppermute | solution.py:643
  118.3 9.2 %collective-permute-start.17 = (bf16[128,2048]{1,0:T(8,128)(2,1)S(1)}, bf16[128,2048]{1,0:T(8,128)(2,1)S(1)}, u32[]{:S(2)}, u32[]{:S(2)}) collective-permute-start(bf16[128,2048]{1,0:T(8,128)(2,1)S(1)} %get-tuple-element.87), channel_id=1, source_target_pairs={{0,8},{4,20},{8,0},{12,28},{16,24},{20,4},{24,16},{28,12},{1,9},{5... | collective-permute-start | bytes 1572872 | tf_op jit(solution)/shard_map/ppermute | solution.py:676
  127.8 9.2 %collective-permute-start.18 = (bf16[256,1024]{1,0:T(8,128)(2,1)S(1)}, bf16[256,1024]{1,0:T(8,128)(2,1)S(1)}, u32[]{:S(2)}, u32[]{:S(2)}) collective-permute-start(bf16[256,1024]{1,0:T(8,128)(2,1)S(1)} %get-tuple-element.90), channel_id=1, source_target_pairs={{0,16},{4,12},{8,24},{12,4},{16,0},{20,28},{24,8},{28,20},{1,17},{... | collective-permute-start | bytes 1572872 | tf_op jit(solution)/shard_map/ppermute | solution.py:676
  129.4 9.5 %collective-permute-start.20 = (bf16[1,32,2048]{2,1,0:T(8,128)(2,1)S(1)}, bf16[1,32,2048]{2,1,0:T(8,128)(2,1)S(1)}, u32[]{:S(2)}, u32[]{:S(2)}) collective-permute-start(bf16[1,32,2048]{2,1,0:T(8,128)(2,1)S(1)} %get-tuple-element.93), channel_id=1, source_target_pairs={{0,1},{1,0},{2,3},{3,2},{4,5},{5,4},{6,7},{7,6},{8,9},{9,8},{10,11... | collective-permute-start | bytes 393224 | tf_op jit(solution)/shard_map/ppermute | solution.py:643
  130.1 12.7 %collective-permute-start.21 = (bf16[1,32,2048]{2,1,0:T(8,128)(2,1)S(1)}, bf16[1,32,2048]{2,1,0:T(8,128)(2,1)S(1)}, u32[]{:S(2)}, u32[]{:S(2)}) collective-permute-start(bf16[1,32,2048]{2,1,0:T(8,128)(2,1)S(1)} %get-tuple-element.94), channel_id=1, source_target_pairs={{0,2},{1,3},{2,0},{3,1},{4,6},{5,7},{6,4},{7,5},{8,10},{9,11},{10,... | collective-permute-start | bytes 393224 | tf_op jit(solution)/shard_map/ppermute | solution.py:643
  132.0 10.9 %collective-permute-start.22 = (bf16[1,32,2048]{2,1,0:T(8,128)(2,1)S(1)}, bf16[1,32,2048]{2,1,0:T(8,128)(2,1)S(1)}, u32[]{:S(2)}, u32[]{:S(2)}) collective-permute-start(bf16[1,32,2048]{2,1,0:T(8,128)(2,1)S(1)} %get-tuple-element.95), channel_id=1, source_target_pairs={{0,3},{1,2},{2,1},{3,0},{4,7},{5,6},{6,5},{7,4},{8,11},{9,10},{10,... | collective-permute-start | bytes 393224 | tf_op jit(solution)/shard_map/ppermute | solution.py:643
  137.2 6.4 %collective-permute-start.19 = (bf16[128,1024]{1,0:T(8,128)(2,1)S(1)}, bf16[128,1024]{1,0:T(8,128)(2,1)S(1)}, u32[]{:S(2)}, u32[]{:S(2)}) collective-permute-start(bf16[128,1024]{1,0:T(8,128)(2,1)S(1)} %get-tuple-element.92), channel_id=1, source_target_pairs={{0,8},{4,20},{8,0},{12,28},{16,24},{20,4},{24,16},{28,12},{1,9},{5... | collective-permute-start | bytes 786440 | tf_op jit(solution)/shard_map/ppermute | solution.py:676
  143.7 10.6 %collective-permute-start.23 = (bf16[1,32,1024]{2,1,0:T(8,128)(2,1)S(1)}, bf16[1,32,1024]{2,1,0:T(8,128)(2,1)S(1)}, u32[]{:S(2)}, u32[]{:S(2)}) collective-permute-start(bf16[1,32,1024]{2,1,0:T(8,128)(2,1)S(1)} %get-tuple-element.98), channel_id=1, source_target_pairs={{0,1},{1,0},{2,3},{3,2},{4,5},{5,4},{6,7},{7,6},{8,9},{9,8},{10,11... | collective-permute-start | bytes 196616 | tf_op jit(solution)/shard_map/ppermute | solution.py:643
  145.2 9.1 %collective-permute-start.24 = (bf16[1,32,1024]{2,1,0:T(8,128)(2,1)S(1)}, bf16[1,32,1024]{2,1,0:T(8,128)(2,1)S(1)}, u32[]{:S(2)}, u32[]{:S(2)}) collective-permute-start(bf16[1,32,1024]{2,1,0:T(8,128)(2,1)S(1)} %get-tuple-element.99), channel_id=1, source_target_pairs={{0,2},{1,3},{2,0},{3,1},{4,6},{5,7},{6,4},{7,5},{8,10},{9,11},{10,... | collective-permute-start | bytes 196616 | tf_op jit(solution)/shard_map/ppermute | solution.py:643
  146.5 7.7 %collective-permute-start.25 = (bf16[1,32,1024]{2,1,0:T(8,128)(2,1)S(1)}, bf16[1,32,1024]{2,1,0:T(8,128)(2,1)S(1)}, u32[]{:S(2)}, u32[]{:S(2)}) collective-permute-start(bf16[1,32,1024]{2,1,0:T(8,128)(2,1)S(1)} %get-tuple-element.100), channel_id=1, source_target_pairs={{0,3},{1,2},{2,1},{3,0},{4,7},{5,6},{6,5},{7,4},{8,11},{9,10},{10,... | collective-permute-start | bytes 196616 | tf_op jit(solution)/shard_map/ppermute | solution.py:643
  (13 other events, 68.3 us)

commit v2 on v1

--- a/solution.py
+++ b/solution.py
@@ -25,7 +25,7 @@
 GATHER_FLOPS = 4 * 10**9
 FINISH_FLOPS = 9 * 10**9
 LANES = 128
-ATTENTION_MIB = 46
+ATTENTION_MIB = 32
 
 NT = (((1,), (1,)), ((), ()))
 TN = (((0,), (0,)), ((), ()))
@@ -743,20 +743,22 @@
     send_2 = grad_rows(rows_send, [dk_2, dv_2], scale, BF)
     received_2 = exchanged(send_2, *first)
     keep_2 = grad_rows(rows_keep, [dk_2, dv_2], scale, F32, after=[send_2])
-    keep, *send = sent_blocks(keep, received, n_lon, [keep_2])
+    keep_2, send_2 = add_split(keep_2, received_2)
+    received_2 = exchanged_stage(send_2, stages[0])
+    grad_inputs, done = input_grads([*dq, dk_1, dk_2, dv_1, dv_2], w_qkv, [send_2])
+    keep, *send = sent_blocks(keep, received, n_lon, [done])
     group_1 = [keep] + [exchanged(a, "lon", i + 1) for i, a in enumerate(send)]
     sum_1 = gather_sums([group_1], [[(0, 2 * width, 0)]], 2 * width, [], GATHER_FLOPS)[None]
-    for stage in stages:
+    for stage in stages[1:]:
         keep_2, send_2 = add_split(keep_2, received_2, [keep])
         received_2 = exchanged_stage(send_2, stage)
-    keep_2, *send_2 = sent_blocks(keep_2, received_2, n_lon, [sum_1])
+    keep_2, *send_2 = sent_blocks(keep_2, received_2, n_lon, [])
     group_2 = [keep_2] + [exchanged(a, "lon", i + 1) for i, a in enumerate(send_2)]
-    grad_inputs, done = input_grads([*dq, dk_1, dk_2, dv_1, dv_2], w_qkv, [keep_2])
     places = [
         [(0, width, 0), (width, half, width), (width + half, half, 2 * width)],
         [(0, half, width + half), (half, half, 2 * width + half)],
     ]
-    grad_w = gather_sums([[sum_1], group_2], places, 3 * width, [done], 10**5)
+    grad_w = gather_sums([[sum_1], group_2], places, 3 * width, [], 10**5)
     return (grad_inputs.reshape(inputs.shape), grad_w)
 
 

time: 155 us -> 154 us (level)
  waiting for transfers between devices: 31.2 us -> 34.4 us
  starting transfers between devices: 45.7 us -> 42.8 us
  Pallas kernels: 71.8 us -> 70.1 us
    ppermute x8, waiting for transfers between devices: 3.94 us -> 11.2 us  [exchanged(): lax.ppermute(array, axis, [(i, i ^ flip) for i in range(lax.axis_size(axi...]
    ppermute x4, waiting for transfers between devices: 10.8 us -> 4.88 us  [exchanged_stage(): return lax.ppermute(array, ('dp', 'lat'), route)]
    ppermute x8, starting transfers between devices: 12.9 us -> 11 us  [exchanged(): lax.ppermute(array, axis, [(i, i ^ flip) for i in range(lax.axis_size(axi...]
    ppermute x6, waiting for transfers between devices: 16.1 us -> 17.9 us  [shifted(): return lax.ppermute(array, axis, route)]
    pallas_call x3, Pallas kernels: 40.9 us -> 39.1 us  [attention_grads(): pl.pallas_call(functools.partial(attention_kernel, band_rows, band_cols,...]
    unnamed x22 -> x16, local copies, waits for them, and re-layouts: 5.27 us -> 5.25 us
  transfers between devices with their start and end apart: 26 -> 26, of which waited for: 9 -> 11; matrix products, arithmetic and copies ran while one was open for 0% -> 0% of each run, Pallas kernels for 29% -> 29%
where the time goes in v2:
time: 154 us
  Pallas kernels  70.1 us (46%)
  starting transfers between devices  42.8 us (28%)
  waiting for transfers between devices  34.4 us (22%)
  local copies, waits for them, and re-layouts  5.25 us (3%)
    pallas_call x3, Pallas kernels, attention_grads(): pl.pallas_call(functools.partial(attention_kernel, band_rows, band_cols,...  39.1 us
    ppermute x6, waiting for transfers between devices, shifted(): return lax.ppermute(array, axis, route)  17.9 us
    pallas_call x21, Pallas kernels, on_chip(): pl.pallas_call(run, in_specs=[pl.BlockSpec(memory_space=pltpu.SMEM)] * le...  16 us
    ppermute x6, starting transfers between devices, shifted(): return lax.ppermute(array, axis, route)  12.8 us
    ppermute x8, starting transfers between devices, swapped(): lax.ppermute(array, axis, route(pairs[offset::2]))  12.5 us
    ppermute x8, waiting for transfers between devices, exchanged(): lax.ppermute(array, axis, [(i, i ^ flip) for i in range(lax.axis_size(axi...  11.2 us
    ppermute x8, starting transfers between devices, exchanged(): lax.ppermute(array, axis, [(i, i ^ flip) for i in range(lax.axis_size(axi...  11 us
    ppermute x4, starting transfers between devices, exchanged_stage(): return lax.ppermute(array, ('dp', 'lat'), route)  6.46 us
  transfers between devices with their start and end apart: 26, of which 11 were waited for; matrix products, arithmetic and copies ran while one was open for 0% of the time, Pallas kernels for 29%

profile of v2, /device:TPU:0, one launch (start us, length us, event | category | flops | bytes accessed | tf_op | source)
XLA Modules:
  0.0 153.6 jit_solution(16882107975031369228)
XLA Ops:
  3.4 5.0 %collective-permute-start.1 = (bf16[192,1024]{1,0:T(8,128)(2,1)}, bf16[192,1024]{1,0:T(8,128)(2,1)S(1)}, u32[]{:S(2)}, u32[]{:S(2)}) collective-permute-start(bf16[192,1024]{1,0:T(8,128)(2,1)} %get-tuple-element.53), channel_id=1, source_target_pairs={{0,3},{1,0},{2,1},{3,2},{4,7},{5,4},{6,5},{7,6},{8,11},{9,8},{10,9... | collective-permute-start | bytes 1179656 | tf_op jit(solution)/shard_map/ppermute | solution.py:629
  13.4 4.0 %shard_map.50.refs_3_.refs_1_ = bf16[8,512,128]{2,1,0:T(8,128)(2,1)} custom-call(s32[3]{0:T(128)} %copy-done.5), custom_call_target="tpu_custom_call" | custom-call | flops 10000000 | bytes 2097152 | tf_op jit(solution)/shard_map/pallas_call | solution.py:70
  17.4 2.8 %copy-done.3 = bf16[1024,3072]{1,0:T(8,128)(2,1)S(1)} copy-done((bf16[1024,3072]{1,0:T(8,128)(2,1)S(1)}, bf16[1024,3072]{1,0:T(8,128)(2,1)}, u32[]{:S(2)}) %copy-start.3) | copy-done | bytes 6291480
  20.2 4.9 %shard_map.53.refs_4_.refs_8_ = bf16[512,3072]{1,0:T(8,128)(2,1)S(1)} custom-call(bf16[512,1024]{1,0:T(8,128)(2,1)S(1)} %bitcast.10, bf16[1024,3072]{1,0:T(8,128)(2,1)S(1)} %copy-done.3, bf16[192,1024]{1,0:T(8,128)(2,1)S(1)} %get-tuple-element.52.refs_2_.refs_0_), custom_call_target="tpu_custom_call" | custom-call | flops 1000000000 | bytes 1048576 | tf_op jit(solution)/shard_map/pallas_call | solution.py:352
  29.1 19.0 %shard_map.56 = (bf16[2,512,256]{2,1,0:T(8,128)(2,1)S(1)}, bf16[2,2,192,256]{3,2,1,0:T(8,128)(2,1)S(1)}, bf16[2,2,192,256]{3,2,1,0:T(8,128)(2,1)S(1)}, bf16[2,2,...) custom-call(s32[3]{0:T(128)S(1)} %copy-done.6, ...), custom_call_target="tpu_custom_call" | custom-call | flops 28000000000 | bytes 16777216 | tf_op jit(solution)/shard_map/pallas_call | solution.py:286
  48.1 6.0 %collective-permute-start.6 = (bf16[2,2,192,256]{3,2,1,0:T(8,128)(2,1)S(1)}, bf16[2,2,192,256]{3,2,1,0:T(8,128)(2,1)S(1)}, u32[]{:S(2)}, u32[]{:S(2)}) collective-permute-start(bf16[2,2,192,256]{3,2,1,0:T(8,128)(2,1)S(1)} %get-tuple-element.66), channel_id=1, source_target_pairs={{0,4},{8,12},{4,0},{12,8},{1,5},{9,13},{5,1},{13,9},{2,6},{10,14},... | collective-permute-start | bytes 1179656 | tf_op jit(solution)/shard_map/ppermute | solution.py:637
  55.0 10.0 %shard_map.57 = (bf16[1,512,256]{2,1,0:T(8,128)(2,1)S(1)}, bf16[1,2,192,256]{3,2,1,0:T(8,128)(2,1)S(1)}, bf16[1,2,192,256]{3,2,1,0:T(8,128)(2,1)S(1)}, bf16[1,2,...) custom-call(s32[3]{0:T(128)S(1)} %copy-done.6, ...), custom_call_target="tpu_custom_call" | custom-call | flops 14000000000 | bytes 8388608 | tf_op jit(solution)/shard_map/pallas_call | solution.py:286
  66.9 2.8 %collective-permute-start.9 = (bf16[2,2,192,256]{3,2,1,0:T(8,128)(2,1)S(1)}, bf16[2,2,192,256]{3,2,1,0:T(8,128)(2,1)S(1)}, u32[]{:S(2)}, u32[]{:S(2)}) collective-permute-start(bf16[2,2,192,256]{3,2,1,0:T(8,128)(2,1)S(1)} %get-tuple-element.68.refs_13_), channel_id=1, source_target_pairs={{0,3},{1,0},{2,1},{3,2},{4,7},{5,4},{6,5},{7,6},{8,11},{9,8},{10,9... | collective-permute-start | bytes 1179656 | tf_op jit(solution)/shard_map/ppermute | solution.py:629
  69.7 10.1 %shard_map.59 = (bf16[1,512,256]{2,1,0:T(8,128)(2,1)S(1)}, bf16[2,2,192,256]{3,2,1,0:T(8,128)(2,1)S(1)}, bf16[2,2,192,256]{3,2,1,0:T(8,128)(2,1)S(1)}, bf16[1,2,...) custom-call(s32[3]{0:T(128)S(1)} %copy-done.6, ...), custom_call_target="tpu_custom_call" | custom-call | flops 14000000000 | bytes 8388608 | tf_op jit(solution)/shard_map/pallas_call | solution.py:286
  82.3 4.2 %collective-permute-done.9.refs_5_ = bf16[2,2,192,256]{3,2,1,0:T(8,128)(2,1)S(1)} collective-permute-done((bf16[2,2,192,256]{3,2,1,0:T(8,128)(2,1)S(1)}, bf16[2,2,192,256]{3,2,1,0:T(8,128)(2,1)S(1)}, u32[]{:S(2)}, u32[]{:S(2)}) %collective-permute-start.9) | collective-permute-done | bytes 393248 | tf_op jit(solution)/shard_map/ppermute | solution.py:629
  86.5 1.9 %shard_map.60 = (bf16[512,512]{1,0:T(8,128)(2,1)S(1)}, bf16[512,512]{1,0:T(8,128)(2,1)S(1)}) custom-call(s32[3]{0:T(128)S(1)} %copy-done.6, bf16[2,2,512,256]{3,2,1,0:T(8,128)(2,1)S(1)} %get-tuple-element.70.refs_1_, bf16[2,2,192,256]{3,2,1,0:T(8,128)(2,1)S(1)} %collective-permute-done.6.refs_3_.refs_2_, ...), custom_call_target="tpu_custom_call" | custom-call | flops 2000000000 | bytes 10000 | tf_op jit(solution)/shard_map/pallas_call | solution.py:327
  90.4 2.1 %collective-permute-start.14 = (bf16[512,2048]{1,0:T(8,128)(2,1)S(1)}, bf16[512,2048]{1,0:T(8,128)(2,1)S(1)}, u32[]{:S(2)}, u32[]{:S(2)}) collective-permute-start(bf16[512,2048]{1,0:T(8,128)(2,1)S(1)} %shard_map.62.refs_6_), channel_id=1, source_target_pairs={{0,4},{4,0},{8,12},{12,8},{1,5},{5,1},{9,13},{13,9},{2,6},{6,2},{1... | collective-permute-start | bytes 6291464 | tf_op jit(solution)/shard_map/ppermute | solution.py:643
  92.5 3.8 %collective-permute-start.13 = (bf16[2,2,192,256]{3,2,1,0:T(8,128)(2,1)S(1)}, bf16[2,2,192,256]{3,2,1,0:T(8,128)(2,1)S(1)}, u32[]{:S(2)}, u32[]{:S(2)}) collective-permute-start(bf16[2,2,192,256]{3,2,1,0:T(8,128)(2,1)S(1)} %get-tuple-element.82.refs_6_), channel_id=1, source_target_pairs={{0,3},{1,0},{2,1},{3,2},{4,7},{5,4},{6,5},{7,6},{8,11},{9,8},{10,9... | collective-permute-start | bytes 1179656 | tf_op jit(solution)/shard_map/ppermute | solution.py:629
  99.6 6.7 %collective-permute-done.12.refs_5_ = bf16[2,2,192,256]{3,2,1,0:T(8,128)(2,1)S(1)} collective-permute-done((bf16[2,2,192,256]{3,2,1,0:T(8,128)(2,1)S(1)}, bf16[2,2,192,256]{3,2,1,0:T(8,128)(2,1)S(1)}, u32[]{:S(2)}, u32[]{:S(2)}) %collective-permute-start.12) | collective-permute-done | bytes 393248 | tf_op jit(solution)/shard_map/ppermute | solution.py:629
  106.3 5.8 %collective-permute-done.13.refs_6_ = bf16[2,2,192,256]{3,2,1,0:T(8,128)(2,1)S(1)} collective-permute-done((bf16[2,2,192,256]{3,2,1,0:T(8,128)(2,1)S(1)}, bf16[2,2,192,256]{3,2,1,0:T(8,128)(2,1)S(1)}, u32[]{:S(2)}, u32[]{:S(2)}) %collective-permute-start.13) | collective-permute-done | bytes 393248 | tf_op jit(solution)/shard_map/ppermute | solution.py:629
  116.4 1.7 %collective-permute-start.17 = (bf16[128,2048]{1,0:T(8,128)(2,1)S(1)}, bf16[128,2048]{1,0:T(8,128)(2,1)S(1)}, u32[]{:S(2)}, u32[]{:S(2)}) collective-permute-start(bf16[128,2048]{1,0:T(8,128)(2,1)S(1)} %get-tuple-element.89), channel_id=1, source_target_pairs={{0,8},{4,20},{8,0},{12,28},{16,24},{20,4},{24,16},{28,12},{1,9},{5... | collective-permute-start | bytes 1572872 | tf_op jit(solution)/shard_map/ppermute | solution.py:676
  120.0 6.1 %shard_map.71 = (bf16[512,1024]{1,0:T(8,128)(2,1)}, f32[8,128]{1,0:T(8,128)S(1)}) custom-call(bf16[2,512,256]{2,1,0:T(8,128)(2,1)S(1)} %get-tuple-element.60.refs_11_.refs_1_.refs_0_, bf16[1,512,256]{2,1,0:T(8,128)(2,1)S(1)} %get-tuple-element.61.refs_5_.refs_2_.refs_1_, bf16[1,512,256]{2,1,0:T(8,128)(2,1)S(1)} %get-tuple-element.69.refs_6_.refs_3_.refs_2_, ...), custom_call_target="tpu_custom_call" | custom-call | flops 4000000000 | bytes 1048576 | tf_op jit(solution)/shard_map/pallas_call | solution.py:390
  126.1 3.8 %collective-permute-done.17.refs_1_ = bf16[128,2048]{1,0:T(8,128)(2,1)S(1)} collective-permute-done((bf16[128,2048]{1,0:T(8,128)(2,1)S(1)}, bf16[128,2048]{1,0:T(8,128)(2,1)S(1)}, u32[]{:S(2)}, u32[]{:S(2)}) %collective-permute-start.17) | collective-permute-done | bytes 524320 | tf_op jit(solution)/shard_map/ppermute | solution.py:676
  130.9 1.7 %collective-permute-start.22 = (bf16[128,1024]{1,0:T(8,128)(2,1)S(1)}, bf16[128,1024]{1,0:T(8,128)(2,1)S(1)}, u32[]{:S(2)}, u32[]{:S(2)}) collective-permute-start(bf16[128,1024]{1,0:T(8,128)(2,1)S(1)} %get-tuple-element.97), channel_id=1, source_target_pairs={{0,8},{4,20},{8,0},{12,28},{16,24},{20,4},{24,16},{28,12},{1,9},{5... | collective-permute-start | bytes 786440 | tf_op jit(solution)/shard_map/ppermute | solution.py:676
  135.2 1.7 %collective-permute-start.20 = (bf16[1,32,2048]{2,1,0:T(8,128)(2,1)S(1)}, bf16[1,32,2048]{2,1,0:T(8,128)(2,1)S(1)}, u32[]{:S(2)}, u32[]{:S(2)}) collective-permute-start(bf16[1,32,2048]{2,1,0:T(8,128)(2,1)S(1)} %get-tuple-element.94), channel_id=1, source_target_pairs={{0,3},{1,2},{2,1},{3,0},{4,7},{5,6},{6,5},{7,4},{8,11},{9,10},{10,... | collective-permute-start | bytes 393224 | tf_op jit(solution)/shard_map/ppermute | solution.py:643
  138.1 2.0 %collective-permute-start.24 = (bf16[1,32,1024]{2,1,0:T(8,128)(2,1)S(1)}, bf16[1,32,1024]{2,1,0:T(8,128)(2,1)S(1)}, u32[]{:S(2)}, u32[]{:S(2)}) collective-permute-start(bf16[1,32,1024]{2,1,0:T(8,128)(2,1)S(1)} %get-tuple-element.100), channel_id=1, source_target_pairs={{0,2},{1,3},{2,0},{3,1},{4,6},{5,7},{6,4},{7,5},{8,10},{9,11},{10,... | collective-permute-start | bytes 196616 | tf_op jit(solution)/shard_map/ppermute | solution.py:643
  140.1 1.7 %collective-permute-start.25 = (bf16[1,32,1024]{2,1,0:T(8,128)(2,1)S(1)}, bf16[1,32,1024]{2,1,0:T(8,128)(2,1)S(1)}, u32[]{:S(2)}, u32[]{:S(2)}) collective-permute-start(bf16[1,32,1024]{2,1,0:T(8,128)(2,1)S(1)} %get-tuple-element.101), channel_id=1, source_target_pairs={{0,3},{1,2},{2,1},{3,0},{4,7},{5,6},{6,5},{7,4},{8,11},{9,10},{10,... | collective-permute-start | bytes 196616 | tf_op jit(solution)/shard_map/ppermute | solution.py:643
  141.8 5.5 %collective-permute-done.19.refs_2_ = bf16[1,32,2048]{2,1,0:T(8,128)(2,1)S(1)} collective-permute-done((bf16[1,32,2048]{2,1,0:T(8,128)(2,1)S(1)}, bf16[1,32,2048]{2,1,0:T(8,128)(2,1)S(1)}, u32[]{:S(2)}, u32[]{:S(2)}) %collective-permute-start.19) | collective-permute-done | bytes 131104 | tf_op jit(solution)/shard_map/ppermute | solution.py:643
  147.4 5.4 %collective-permute-done.24.refs_3_ = bf16[1,32,1024]{2,1,0:T(8,128)(2,1)S(1)} collective-permute-done((bf16[1,32,1024]{2,1,0:T(8,128)(2,1)S(1)}, bf16[1,32,1024]{2,1,0:T(8,128)(2,1)S(1)}, u32[]{:S(2)}, u32[]{:S(2)}) %collective-permute-start.24) | collective-permute-done | bytes 65568 | tf_op jit(solution)/shard_map/ppermute | solution.py:643
  (72 shorter events, 33.9 us)
Async XLA Ops:
  3.4 21.7 %collective-permute-start.1 = (bf16[192,1024]{1,0:T(8,128)(2,1)}, bf16[192,1024]{1,0:T(8,128)(2,1)S(1)}, u32[]{:S(2)}, u32[]{:S(2)}) collective-permute-start(bf16[192,1024]{1,0:T(8,128)(2,1)} %get-tuple-element.53), channel_id=1, source_target_pairs={{0,3},{1,0},{2,1},{3,2},{4,7},{5,4},{6,5},{7,6},{8,11},{9,8},{10,9... | collective-permute-start | bytes 1179656 | tf_op jit(solution)/shard_map/ppermute | solution.py:629
  8.4 17.9 %collective-permute-start = (bf16[192,1024]{1,0:T(8,128)(2,1)S(1)}, bf16[192,1024]{1,0:T(8,128)(2,1)S(1)}, u32[]{:S(2)}, u32[]{:S(2)}) collective-permute-start(bf16[192,1024]{1,0:T(8,128)(2,1)S(1)} %get-tuple-element.52.refs_2_.refs_0_), channel_id=1, source_target_pairs={{0,1},{1,2},{2,3},{3,0},{4,5},{5,6},{6,7},{7,4},{8,9},{9,10},{10,1... | collective-permute-start | bytes 1179656 | tf_op jit(solution)/shard_map/ppermute | solution.py:629
  11.0 17.7 %collective-permute-start.2 = (bf16[96,1024]{1,0:T(8,128)(2,1)}, bf16[96,1024]{1,0:T(8,128)(2,1)S(1)}, u32[]{:S(2)}, u32[]{:S(2)}) collective-permute-start(bf16[96,1024]{1,0:T(8,128)(2,1)} %get-tuple-element.54), channel_id=1, source_target_pairs={{0,4},{8,12},{4,0},{12,8},{1,5},{9,13},{5,1},{13,9},{2,6},{10,14},... | collective-permute-start | bytes 589832 | tf_op jit(solution)/shard_map/ppermute | solution.py:637
  11.0 17.7 %collective-permute-start.3 = (bf16[96,1024]{1,0:T(8,128)(2,1)}, bf16[96,1024]{1,0:T(8,128)(2,1)}, u32[]{:S(2)}, u32[]{:S(2)}) collective-permute-start(bf16[96,1024]{1,0:T(8,128)(2,1)} %get-tuple-element.55), channel_id=1, source_target_pairs={{4,8},{8,4},{5,9},{9,5},{6,10},{10,6},{7,11},{11,7},{20,24},{24,20... | collective-permute-start | bytes 589832 | tf_op jit(solution)/shard_map/ppermute | solution.py:637
  48.1 16.9 %collective-permute-start.6 = (bf16[2,2,192,256]{3,2,1,0:T(8,128)(2,1)S(1)}, bf16[2,2,192,256]{3,2,1,0:T(8,128)(2,1)S(1)}, u32[]{:S(2)}, u32[]{:S(2)}) collective-permute-start(bf16[2,2,192,256]{3,2,1,0:T(8,128)(2,1)S(1)} %get-tuple-element.66), channel_id=1, source_target_pairs={{0,4},{8,12},{4,0},{12,8},{1,5},{9,13},{5,1},{13,9},{2,6},{10,14},... | collective-permute-start | bytes 1179656 | tf_op jit(solution)/shard_map/ppermute | solution.py:637
  54.1 10.9 %collective-permute-start.7 = (bf16[2,2,192,256]{3,2,1,0:T(8,128)(2,1)S(1)}, bf16[2,2,192,256]{3,2,1,0:T(8,128)(2,1)S(1)}, u32[]{:S(2)}, u32[]{:S(2)}) collective-permute-start(bf16[2,2,192,256]{3,2,1,0:T(8,128)(2,1)S(1)} %get-tuple-element.67), channel_id=1, source_target_pairs={{4,8},{8,4},{5,9},{9,5},{6,10},{10,6},{7,11},{11,7},{20,24},{24,20... | collective-permute-start | bytes 1179656 | tf_op jit(solution)/shard_map/ppermute | solution.py:637
  65.7 16.6 %collective-permute-start.8 = (bf16[2,2,192,256]{3,2,1,0:T(8,128)(2,1)S(1)}, bf16[2,2,192,256]{3,2,1,0:T(8,128)(2,1)S(1)}, u32[]{:S(2)}, u32[]{:S(2)}) collective-permute-start(bf16[2,2,192,256]{3,2,1,0:T(8,128)(2,1)S(1)} %get-tuple-element.71), channel_id=1, source_target_pairs={{0,1},{1,2},{2,3},{3,0},{4,5},{5,6},{6,7},{7,4},{8,9},{9,10},{10,1... | collective-permute-start | bytes 1179656 | tf_op jit(solution)/shard_map/ppermute | solution.py:629
  66.9 19.6 %collective-permute-start.9 = (bf16[2,2,192,256]{3,2,1,0:T(8,128)(2,1)S(1)}, bf16[2,2,192,256]{3,2,1,0:T(8,128)(2,1)S(1)}, u32[]{:S(2)}, u32[]{:S(2)}) collective-permute-start(bf16[2,2,192,256]{3,2,1,0:T(8,128)(2,1)S(1)} %get-tuple-element.68.refs_13_), channel_id=1, source_target_pairs={{0,3},{1,0},{2,1},{3,2},{4,7},{5,4},{6,5},{7,6},{8,11},{9,8},{10,9... | collective-permute-start | bytes 1179656 | tf_op jit(solution)/shard_map/ppermute | solution.py:629
  79.7 8.7 %collective-permute-start.10 = (bf16[2,2,192,256]{3,2,1,0:T(8,128)(2,1)S(1)}, bf16[2,2,192,256]{3,2,1,0:T(8,128)(2,1)S(1)}, u32[]{:S(2)}, u32[]{:S(2)}) collective-permute-start(bf16[2,2,192,256]{3,2,1,0:T(8,128)(2,1)S(1)} %get-tuple-element.75), channel_id=1, source_target_pairs={{0,4},{8,12},{4,0},{12,8},{1,5},{9,13},{5,1},{13,9},{2,6},{10,14},... | collective-permute-start | bytes 1179656 | tf_op jit(solution)/shard_map/ppermute | solution.py:637
  81.4 7.0 %collective-permute-start.11 = (bf16[2,2,192,256]{3,2,1,0:T(8,128)(2,1)S(1)}, bf16[2,2,192,256]{3,2,1,0:T(8,128)(2,1)S(1)}, u32[]{:S(2)}, u32[]{:S(2)}) collective-permute-start(bf16[2,2,192,256]{3,2,1,0:T(8,128)(2,1)S(1)} %get-tuple-element.76), channel_id=1, source_target_pairs={{4,8},{8,4},{5,9},{9,5},{6,10},{10,6},{7,11},{11,7},{20,24},{24,20... | collective-permute-start | bytes 1179656 | tf_op jit(solution)/shard_map/ppermute | solution.py:637
  90.4 7.2 %collective-permute-start.14 = (bf16[512,2048]{1,0:T(8,128)(2,1)S(1)}, bf16[512,2048]{1,0:T(8,128)(2,1)S(1)}, u32[]{:S(2)}, u32[]{:S(2)}) collective-permute-start(bf16[512,2048]{1,0:T(8,128)(2,1)S(1)} %shard_map.62.refs_6_), channel_id=1, source_target_pairs={{0,4},{4,0},{8,12},{12,8},{1,5},{5,1},{9,13},{13,9},{2,6},{6,2},{1... | collective-permute-start | bytes 6291464 | tf_op jit(solution)/shard_map/ppermute | solution.py:643
  92.5 13.8 %collective-permute-start.12 = (bf16[2,2,192,256]{3,2,1,0:T(8,128)(2,1)S(1)}, bf16[2,2,192,256]{3,2,1,0:T(8,128)(2,1)S(1)}, u32[]{:S(2)}, u32[]{:S(2)}) collective-permute-start(bf16[2,2,192,256]{3,2,1,0:T(8,128)(2,1)S(1)} %get-tuple-element.81), channel_id=1, source_target_pairs={{0,1},{1,2},{2,3},{3,0},{4,5},{5,6},{6,7},{7,4},{8,9},{9,10},{10,1... | collective-permute-start | bytes 1179656 | tf_op jit(solution)/shard_map/ppermute | solution.py:629
  92.5 19.6 %collective-permute-start.13 = (bf16[2,2,192,256]{3,2,1,0:T(8,128)(2,1)S(1)}, bf16[2,2,192,256]{3,2,1,0:T(8,128)(2,1)S(1)}, u32[]{:S(2)}, u32[]{:S(2)}) collective-permute-start(bf16[2,2,192,256]{3,2,1,0:T(8,128)(2,1)S(1)} %get-tuple-element.82.refs_6_), channel_id=1, source_target_pairs={{0,3},{1,0},{2,1},{3,2},{4,7},{5,4},{6,5},{7,6},{8,11},{9,8},{10,9... | collective-permute-start | bytes 1179656 | tf_op jit(solution)/shard_map/ppermute | solution.py:629
  98.1 15.3 %collective-permute-start.15 = (bf16[256,2048]{1,0:T(8,128)(2,1)S(1)}, bf16[256,2048]{1,0:T(8,128)(2,1)S(1)}, u32[]{:S(2)}, u32[]{:S(2)}) collective-permute-start(bf16[256,2048]{1,0:T(8,128)(2,1)S(1)} %get-tuple-element.85), channel_id=1, source_target_pairs={{0,16},{4,12},{8,24},{12,4},{16,0},{20,28},{24,8},{28,20},{1,17},{... | collective-permute-start | bytes 3145736 | tf_op jit(solution)/shard_map/ppermute | solution.py:676
  115.6 2.7 %collective-permute-start.16 = (bf16[512,1024]{1,0:T(8,128)(2,1)S(1)}, bf16[512,1024]{1,0:T(8,128)(2,1)S(1)}, u32[]{:S(2)}, u32[]{:S(2)}) collective-permute-start(bf16[512,1024]{1,0:T(8,128)(2,1)S(1)} %shard_map.68.refs_3_), channel_id=1, source_target_pairs={{0,4},{4,0},{8,12},{12,8},{1,5},{5,1},{9,13},{13,9},{2,6},{6,2},{1... | collective-permute-start | bytes 3145736 | tf_op jit(solution)/shard_map/ppermute | solution.py:643
  116.4 13.5 %collective-permute-start.17 = (bf16[128,2048]{1,0:T(8,128)(2,1)S(1)}, bf16[128,2048]{1,0:T(8,128)(2,1)S(1)}, u32[]{:S(2)}, u32[]{:S(2)}) collective-permute-start(bf16[128,2048]{1,0:T(8,128)(2,1)S(1)} %get-tuple-element.89), channel_id=1, source_target_pairs={{0,8},{4,20},{8,0},{12,28},{16,24},{20,4},{24,16},{28,12},{1,9},{5... | collective-permute-start | bytes 1572872 | tf_op jit(solution)/shard_map/ppermute | solution.py:676
  118.5 12.3 %collective-permute-start.21 = (bf16[256,1024]{1,0:T(8,128)(2,1)S(1)}, bf16[256,1024]{1,0:T(8,128)(2,1)S(1)}, u32[]{:S(2)}, u32[]{:S(2)}) collective-permute-start(bf16[256,1024]{1,0:T(8,128)(2,1)S(1)} %get-tuple-element.87.refs_8_), channel_id=1, source_target_pairs={{0,16},{4,12},{8,24},{12,4},{16,0},{20,28},{24,8},{28,20},{1,17},{... | collective-permute-start | bytes 1572872 | tf_op jit(solution)/shard_map/ppermute | solution.py:676
  130.9 6.4 %collective-permute-start.22 = (bf16[128,1024]{1,0:T(8,128)(2,1)S(1)}, bf16[128,1024]{1,0:T(8,128)(2,1)S(1)}, u32[]{:S(2)}, u32[]{:S(2)}) collective-permute-start(bf16[128,1024]{1,0:T(8,128)(2,1)S(1)} %get-tuple-element.97), channel_id=1, source_target_pairs={{0,8},{4,20},{8,0},{12,28},{16,24},{20,4},{24,16},{28,12},{1,9},{5... | collective-permute-start | bytes 786440 | tf_op jit(solution)/shard_map/ppermute | solution.py:676
  132.5 7.5 %collective-permute-start.18 = (bf16[1,32,2048]{2,1,0:T(8,128)(2,1)S(1)}, bf16[1,32,2048]{2,1,0:T(8,128)(2,1)S(1)}, u32[]{:S(2)}, u32[]{:S(2)}) collective-permute-start(bf16[1,32,2048]{2,1,0:T(8,128)(2,1)S(1)} %get-tuple-element.92), channel_id=1, source_target_pairs={{0,1},{1,0},{2,3},{3,2},{4,5},{5,4},{6,7},{7,6},{8,9},{9,8},{10,11... | collective-permute-start | bytes 393224 | tf_op jit(solution)/shard_map/ppermute | solution.py:643
  133.6 13.7 %collective-permute-start.19 = (bf16[1,32,2048]{2,1,0:T(8,128)(2,1)S(1)}, bf16[1,32,2048]{2,1,0:T(8,128)(2,1)S(1)}, u32[]{:S(2)}, u32[]{:S(2)}) collective-permute-start(bf16[1,32,2048]{2,1,0:T(8,128)(2,1)S(1)} %get-tuple-element.93), channel_id=1, source_target_pairs={{0,2},{1,3},{2,0},{3,1},{4,6},{5,7},{6,4},{7,5},{8,10},{9,11},{10,... | collective-permute-start | bytes 393224 | tf_op jit(solution)/shard_map/ppermute | solution.py:643
  135.2 12.1 %collective-permute-start.20 = (bf16[1,32,2048]{2,1,0:T(8,128)(2,1)S(1)}, bf16[1,32,2048]{2,1,0:T(8,128)(2,1)S(1)}, u32[]{:S(2)}, u32[]{:S(2)}) collective-permute-start(bf16[1,32,2048]{2,1,0:T(8,128)(2,1)S(1)} %get-tuple-element.94), channel_id=1, source_target_pairs={{0,3},{1,2},{2,1},{3,0},{4,7},{5,6},{6,5},{7,4},{8,11},{9,10},{10,... | collective-permute-start | bytes 393224 | tf_op jit(solution)/shard_map/ppermute | solution.py:643
  137.3 10.0 %collective-permute-start.23 = (bf16[1,32,1024]{2,1,0:T(8,128)(2,1)S(1)}, bf16[1,32,1024]{2,1,0:T(8,128)(2,1)S(1)}, u32[]{:S(2)}, u32[]{:S(2)}) collective-permute-start(bf16[1,32,1024]{2,1,0:T(8,128)(2,1)S(1)} %get-tuple-element.99), channel_id=1, source_target_pairs={{0,1},{1,0},{2,3},{3,2},{4,5},{5,4},{6,7},{7,6},{8,9},{9,8},{10,11... | collective-permute-start | bytes 196616 | tf_op jit(solution)/shard_map/ppermute | solution.py:643
  138.1 14.7 %collective-permute-start.24 = (bf16[1,32,1024]{2,1,0:T(8,128)(2,1)S(1)}, bf16[1,32,1024]{2,1,0:T(8,128)(2,1)S(1)}, u32[]{:S(2)}, u32[]{:S(2)}) collective-permute-start(bf16[1,32,1024]{2,1,0:T(8,128)(2,1)S(1)} %get-tuple-element.100), channel_id=1, source_target_pairs={{0,2},{1,3},{2,0},{3,1},{4,6},{5,7},{6,4},{7,5},{8,10},{9,11},{10,... | collective-permute-start | bytes 196616 | tf_op jit(solution)/shard_map/ppermute | solution.py:643
  140.1 12.7 %collective-permute-start.25 = (bf16[1,32,1024]{2,1,0:T(8,128)(2,1)S(1)}, bf16[1,32,1024]{2,1,0:T(8,128)(2,1)S(1)}, u32[]{:S(2)}, u32[]{:S(2)}) collective-permute-start(bf16[1,32,1024]{2,1,0:T(8,128)(2,1)S(1)} %get-tuple-element.101), channel_id=1, source_target_pairs={{0,3},{1,2},{2,1},{3,0},{4,7},{5,6},{6,5},{7,4},{8,11},{9,10},{10,... | collective-permute-start | bytes 196616 | tf_op jit(solution)/shard_map/ppermute | solution.py:643
  (10 other events, 42.7 us)
